TPU v7x, 128 devices: a whole 4x4x4 slice. The times are simulated.
128 devices in a mesh: pb: 16 (over z, y), pa: 8 (over x, core).
Axes of the slice: x: 4, y: 4, z: 4, core: 2. Of those that a mesh axis runs over, the one named last changes fastest.
Arguments:
- hidden_in: bfloat16 [32768, 2048], P(('pb', 'pa')), may hold values from -6 to 6
- norm_gain: float32 [2048], replicated, may hold values from 0.1 to 1.9
- query_weight: bfloat16 [2048, 2048], replicated, may hold values from -0.125 to 0.125
- out_weight: bfloat16 [2048, 2048], replicated, may hold values from -0.125 to 0.125
- corpus_kv: bfloat16 [128, 64, 4096], P('pb'), may hold values from -24 to 24
- owner_ids: int32 [16, 8, 8, 2, 1], P('pb', 'pa'), may hold values from 0 to 15; in each aligned block of 16 rows (0 to 15, 16 to 31, ..., all dimensions but the last counted through in order) at most 2 rows name the same one
- local_ids: int32 [16, 8, 8, 2], P('pb', 'pa'), may hold values from 0 to 7
- counts: int32 [128], P('pb'), may hold values from 1 to 16
Outputs:
- update: bfloat16 [32768, 2048], P(('pb', 'pa'))
Inputs may be any that keep to these rules, and one draw needn't show every extreme that they name: `owner_ids`: among the 16 slots of one device (one entry [b, p]), no corpus shard is named more than 2 times, a bound that some block reaches.
All inputs are finite; a program needn't handle non-finite values.
Results may differ from a plain program's by a relative error of at most 0.011.
The roundings to bfloat16 on the way count: a program that leaves them out, or rounds other values in their place, can miss the bound.
Values may be sent and summed in bfloat16 or wider, within the bound.
No kernel may reach another device: no remote copies, remote signals or barrier semaphores. Data moves between devices by JAX's collectives and lax.ppermute only.
A program may use at most 320 MiB of HBM per device.

v0:
```python
import jax
import jax.numpy as jnp
from jax import lax
from jax.sharding import PartitionSpec as P

DH = 64
Q_GRP = 8
P_SIZE = 64
TQ = 256


def scaled_norm(hidden_in, norm_gain):
    widened = hidden_in.astype(jnp.float32)
    factor = lax.rsqrt(jnp.mean(widened * widened, axis=-1, keepdims=True) + 1e-06)
    return (widened * factor * norm_gain).astype(jnp.bfloat16)


def attend(query_block, key_rows, value_rows, live_keys, reduce_top):
    scores = jnp.einsum(
        "jthd,jkhd->jhtk", query_block, key_rows, preferred_element_type=jnp.float32
    )
    scores = jnp.where(live_keys[:, None, None, :], scores, -1e30)
    row_top = reduce_top(jnp.max(scores, axis=-1))
    exp_scores = jnp.where(live_keys[:, None, None, :], jnp.exp(scores - row_top[..., None]), 0.0)
    totals = jnp.sum(exp_scores, axis=-1)
    numerators = jnp.einsum(
        "jhtk,jkhd->jthd",
        exp_scores.astype(jnp.bfloat16),
        value_rows,
        preferred_element_type=jnp.float32,
    )
    return (numerators, totals)


def fetch_whole(corpus_kv, request_table, target, group_count, capacity, model_width):
    found = corpus_kv[lax.all_to_all(request_table, "pb", split_axis=0, concat_axis=0, tiled=True)]
    replies = lax.all_to_all(found, "pb", split_axis=0, concat_axis=0, tiled=True)
    return replies.reshape(group_count * capacity, P_SIZE, 2 * model_width)[target]


def body(hidden_in, norm_gain, query_weight, out_weight, corpus_kv, owner_ids, local_ids, counts):
    group_count = lax.axis_size("pb")
    column_index = lax.axis_index("pa")
    model_width = hidden_in.shape[1]
    head_count = model_width // DH
    local_slots = owner_ids.shape[3]
    owners = owner_ids.reshape(-1)
    wanted = local_ids.reshape(-1)
    slot_count = owners.shape[0]
    capacity = 2 * slot_count // group_count
    same_owner = owners[:, None] == owners[None, :]
    before = jnp.arange(slot_count)[None, :] < jnp.arange(slot_count)[:, None]
    position = jnp.sum((same_owner & before).astype(jnp.int32), axis=1)
    target = owners * capacity + position
    onehot = target[:, None] == jnp.arange(group_count * capacity)[None, :]
    request_table = jnp.sum(jnp.where(onehot, wanted[:, None], 0), axis=0)
    request_table = request_table.reshape(group_count, capacity)
    normed = scaled_norm(hidden_in, norm_gain)
    queries = jnp.dot(normed, query_weight, preferred_element_type=jnp.float32).astype(jnp.bfloat16)
    fetched = fetch_whole(corpus_kv, request_table, target, group_count, capacity, model_width)
    fetched = fetched.reshape(Q_GRP, local_slots, P_SIZE, 2 * model_width)
    group_queries = lax.all_gather(queries, "pa", axis=0, tiled=True)
    query_block = group_queries.reshape(Q_GRP, TQ, head_count, DH)
    key_rows = fetched[..., :model_width].reshape(Q_GRP, local_slots * P_SIZE, head_count, DH)
    value_rows = fetched[..., model_width:].reshape(Q_GRP, local_slots * P_SIZE, head_count, DH)
    slot_number = column_index * local_slots + jnp.arange(local_slots, dtype=jnp.int32)
    live_slots = slot_number[None, :] < counts[:, None]
    live_keys = jnp.broadcast_to(live_slots[:, :, None], (Q_GRP, local_slots, P_SIZE)).reshape(
        Q_GRP, local_slots * P_SIZE
    )
    numerators, totals = attend(
        query_block, key_rows, value_rows, live_keys, lambda value: lax.pmax(value, "pa")
    )
    numerators = numerators.reshape(Q_GRP * TQ, model_width)
    totals = jnp.transpose(totals, (0, 2, 1)).reshape(Q_GRP * TQ, head_count)
    share_num, share_tot = (
        lax.psum_scatter(numerators, "pa", scatter_dimension=0, tiled=True),
        lax.psum_scatter(totals, "pa", scatter_dimension=0, tiled=True),
    )
    attended = (share_num.reshape(-1, head_count, DH) / share_tot[:, :, None]).reshape(
        -1, model_width
    )
    attended = attended.astype(jnp.bfloat16)
    return jnp.dot(attended, out_weight, preferred_element_type=jnp.float32).astype(jnp.bfloat16)


def solution(mesh):
    placed = (
        P(("pb", "pa"), None),
        P(),
        P(),
        P(),
        P("pb", None, None),
        P("pb", "pa", None, None, None),
        P("pb", "pa", None, None),
        P("pb"),
    )
    return jax.shard_map(
        body, mesh=mesh, in_specs=placed, out_specs=P(("pb", "pa"), None), check_vma=False
    )
```

profile of v0, /device:TPU:0, one launch (start us, length us, event | category | flops | bytes accessed | tf_op | source)
XLA Modules:
  0.0 578.1 jit_solution(10317717416719594736)
XLA Ops:
  6.5 0.8 copy.52
  7.3 0.1 reshape.139
  7.4 0.2 convert_reduce_fusion
  7.6 0.8 copy.53
  8.3 0.1 broadcast_in_dim.52
  8.4 0.1 select_reduce_fusion.1
  8.5 0.1 all_to_all.11
  8.6 15.5 %all_to_all.17 = s32[16,1,2]{2,1,0:T(1,128)S(1)} all-to-all(s32[16,1,2]{2,1,0:T(1,128)S(1)} %bitcast.51), channel_id=1, replica_groups=mesh['pb'=16,'pa'=8] {'pb'}, dimensions={0} | all-to-all | bytes 256 | tf_op jit(solution)/shard_map/all_to_all | solution.py:36
  24.1 0.1 copy.55
  24.2 0.1 copy.56
  24.2 0.1 reshape.149
  24.3 9.3 %gather_fusion = bf16[32,64,4096]{2,1,0:T(8,128)(2,1)} fusion(bf16[8,64,4096]{2,1,0:T(8,128)(2,1)} %param.12, s32[1024]{0:T(1024)S(1)} %pad_clamp_fusion.1), kind=kCustom, calls=%fused_computation | custom fusion | bytes 33554560 | tf_op jit(solution)/shard_map/gather | solution.py:36
  33.6 0.0 copy-start.1
  33.6 0.0 copy-start.4
  33.6 5.3 all-to-all-start.1
  38.9 0.0 all-gather.2.cloned.1.call-start
  39.0 0.0 copy-done.1
  39.0 0.3 fusion.15
  39.3 0.0 copy-done.4
  39.3 0.0 copy-start.2
  39.3 0.0 copy-start.3
  39.3 6.7 %convolution_convert_fusion.1 = bf16[256,2048]{1,0:T(8,128)(2,1)} fusion(bf16[2048,2048]{1,0:T(8,128)(2,1)} %param.10, bf16[256,2048]{1,0:T(8,128)(2,1)S(1)} %copy-done.1, f32[2048]{0:T(1024)S(1)} %copy-done.4, f32[256]{0:T(256)S(1)} %add_rsqrt_fusion), kind=kOutput, calls=%fused_computation.19 | convolution fusion | flops 2150105088 | bytes 10494976 | tf_op jit(solution)/shard_map/dot_general | solution.py:59
  46.0 0.0 all-gather.2.cloned.1.call-update
  46.1 0.0 all-reduce.2.cloned.1.call-start
  46.1 0.0 copy-done.2
  46.1 0.1 copy.57
  46.2 0.1 mul.42
  46.3 0.0 copy-done.3
  46.3 0.1 broadcast_compare_fusion
  46.4 0.1 broadcast_in_dim.55
  46.5 0.1 broadcast_in_dim.56
  46.6 50.8 %all-gather.2.cloned.1.call-done = bf16[2048,2048]{1,0:T(8,128)(2,1)} async-done(((bf16[256,2048]{1,0:T(8,128)(2,1)}), bf16[2048,2048]{1,0:T(8,128)(2,1)}) %all-gather.2.cloned.1.call-update) | async-done | bytes 8388624 | tf_op jit(solution)/shard_map/all_gather | solution.py:62
  97.4 24.4 %reshape.164 = bf16[8,256,32,64]{3,2,1,0:T(8,128)(2,1)} reshape(bf16[2048,2048]{1,0:T(8,128)(2,1)} %all-gather.2.cloned.1.call-done) | data formatting | bytes 16777216 | tf_op jit(solution)/shard_map/reshape | solution.py:63
  121.8 161.0 %all-to-all-done.1 = bf16[16,2,64,4096]{3,2,1,0:T(8,128)(2,1)} async-done(((bf16[16,2,64,4096]{3,2,1,0:T(8,128)(2,1)}), bf16[16,2,64,4096]{3,2,1,0:T(8,128)(2,1)}, u32[]{:S(2)}, u32[]{:S(2)}) %all-to-all-start.1) | async-done | bytes 16777248 | tf_op jit(solution)/shard_map/all_to_all | solution.py:37
  282.8 10.5 %gather_fusion.1 = bf16[16,64,4096]{2,1,0:T(8,128)(2,1)} fusion(bf16[32,64,4096]{2,1,0:T(8,128)(2,1)} %bitcast.3, s32[1024]{0:T(1024)S(1)} %pad_clamp_fusion), kind=kCustom, calls=%fused_computation.1 | custom fusion | bytes 16777280 | tf_op jit(solution)/shard_map/gather | solution.py:38
  293.3 6.1 %fusion.26 = (bf16[8,2,64,2048]{3,2,1,0:T(8,128)(2,1)}, bf16[8,2,64,2048]{3,2,1,0:T(8,128)(2,1)}) fusion(bf16[8,2,64,4096]{3,2,1,0:T(8,128)(2,1)} %bitcast.48), kind=kLoop, calls=%fused_computation.45 | loop fusion | bytes 16777216 | tf_op jit(solution)/shard_map/slice | solution.py:65
  299.4 12.8 %reshape.144 = bf16[8,128,32,64]{3,2,1,0:T(8,128)(2,1)} reshape(bf16[8,2,64,2048]{3,2,1,0:T(8,128)(2,1)} %get-tuple-element.6) | data formatting | bytes 8388608 | tf_op jit(solution)/shard_map/reshape | solution.py:64
  312.2 30.1 %select_reduce_fusion = (f32[8,32,256]{2,1,0:T(8,128)}, f32[8,32,256,128]{2,3,1,0:T(8,128)}) fusion(pred[8,128]{1,0:T(8,128)(4,1)S(1)} %broadcast_in_dim.56, bf16[8,128,32,64]{3,2,1,0:T(8,128)(2,1)} %reshape.144, bf16[8,256,32,64]{3,2,1,0:T(8,128)(2,1)} %reshape.164), kind=kOutput, calls=%fused_computation.3 | convolution fusion | flops 1090453504 | bytes 46400512 | tf_op jit(solution)/shard_map/jthd,jkhd->jhtk/dot_general | solution.py:19
  342.3 0.0 all-reduce.2.cloned.1.call-update
  342.3 0.2 reduce-scatter.5.cloned.1.call-start
  342.5 12.8 %reshape.142 = bf16[8,128,32,64]{3,2,1,0:T(8,128)(2,1)} reshape(bf16[8,2,64,2048]{3,2,1,0:T(8,128)(2,1)} %get-tuple-element.5) | data formatting | bytes 8388608 | tf_op jit(solution)/shard_map/reshape | solution.py:65
  355.4 47.7 %all-reduce.2.cloned.1.call-done = f32[8,32,256]{2,1,0:T(8,128)} async-done(((f32[8,32,256]{2,1,0:T(8,128)}), f32[8,32,256]{2,1,0:T(8,128)}) %all-reduce.2.cloned.1.call-update) | async-done | bytes 262160 | tf_op jit(solution)/shard_map/pmax | solution.py:72
  403.1 0.0 copy-start
  403.1 15.4 %fusion = f32[8,32,256]{2,1,0:T(8,128)S(1)} fusion(f32[8,32,256,128]{2,3,1,0:T(8,128)} %get-tuple-element.8, f32[8,32,256]{2,1,0:T(8,128)} %all-reduce.2.cloned.1.call-done, pred[8,128]{1,0:T(8,128)(4,1)S(1)} %broadcast_in_dim.56), kind=kLoop, calls=%fused_computation.4 | loop fusion | flops 33488896 | bytes 34079744 | tf_op jit(solution)/shard_map/reduce_sum | solution.py:25
  418.6 0.7 copy.68
  419.3 0.0 reduce-scatter.5.cloned.1.call-update
  419.3 0.0 reduce-scatter.3.cloned.1.call-start
  419.4 0.0 copy-done
  419.4 24.1 %fusion.10 = f32[8,256,32,64]{1,3,2,0:T(8,128)} fusion(f32[8,32,256,128]{2,3,1,0:T(8,128)} %get-tuple-element.8, f32[8,32,256]{2,1,0:T(8,128)S(1)} %copy-done, pred[8,128]{1,0:T(8,128)(4,1)S(1)} %broadcast_in_dim.56, bf16[8,128,32,64]{3,2,1,0:T(8,128)(2,1)} %reshape.142), kind=kOutput, calls=%fused_computation.13 | convolution fusion | flops 1107296256 | bytes 54789120 | tf_op jit(solution)/shard_map/jhtk,jkhd->jthd/dot_general | solution.py:26
  443.5 17.4 %copy.63 = f32[8,256,32,64]{1,0,3,2:T(8,128)S(1)} copy(f32[8,256,32,64]{1,3,2,0:T(8,128)} %fusion.10) | data formatting | bytes 33554432 | tf_op jit(solution)/shard_map/jhtk,jkhd->jthd/transpose | solution.py:26
  460.9 11.2 %copy.69 = f32[256,8,8,256]{3,1,2,0:T(8,128)} copy(f32[256,8,8,256]{3,2,1,0:T(8,128)S(1)} %bitcast.47) | data formatting | bytes 33554432
  472.1 0.0 reduce-scatter.3.cloned.1.call-update
  472.2 0.0 reduce-scatter.5.cloned.1.call-done
  472.2 90.9 %reduce-scatter.3.cloned.1.call-done = f32[256,2048]{0,1:T(8,128)} async-done(((f32[2048,2048]{0,1:T(8,128)}), f32[256,2048]{0,1:T(8,128)}) %reduce-scatter.3.cloned.1.call-update) | async-done | bytes 2097168 | tf_op jit(solution)/shard_map/reduce_scatter | solution.py:77
  563.1 1.8 fusion.18
  564.9 6.7 %convolution_convert_fusion = bf16[256,2048]{1,0:T(8,128)(2,1)} fusion(bf16[256,2048]{0,1:T(8,128)(2,1)S(1)} %fusion.18, bf16[2048,2048]{1,0:T(8,128)(2,1)} %param.11), kind=kOutput, calls=%fused_computation.18 | convolution fusion | flops 2148007936 | bytes 10485760 | tf_op jit(solution)/shard_map/dot_general | solution.py:84
  (8 shorter events, 0.0 us)
Async XLA Ops:
  33.6 5.4 copy-start.1
  33.6 5.7 copy-start.4
  33.6 249.1 %all-to-all-start.1 = ((bf16[16,2,64,4096]{3,2,1,0:T(8,128)(2,1)}), bf16[16,2,64,4096]{3,2,1,0:T(8,128)(2,1)}, u32[]{:S(2)}, u32[]{:S(2)}) async-start(bf16[16,2,64,4096]{3,2,1,0:T(8,128)(2,1)} %bitcast.45), calls=%async_computation.1 | async-start | bytes 33554432 | tf_op jit(solution)/shard_map/all_to_all | solution.py:37
  38.9 58.5 %all-gather.2.cloned.1.call-start = ((), (), s32[]{:S(2)}) async-start(), calls=%async_computation.4 | async-start | bytes 9437184 | tf_op jit(solution)/shard_map/all_gather | solution.py:62
  39.3 6.9 %copy-start.2 = (s32[1,1,8,2,1]{2,4,3,1,0:T(1,128)S(1)}, s32[1,1,8,2,1]{2,4,3,1,0:T(1,128)}, u32[]{:S(2)}) copy-start(s32[1,1,8,2,1]{2,4,3,1,0:T(1,128)} %param.13) | copy-start | bytes 196
  39.3 7.0 %copy-start.3 = (s32[8]{0:T(128)S(1)}, s32[8]{0:T(128)}, u32[]{:S(2)}) copy-start(s32[8]{0:T(128)} %param.15) | copy-start | bytes 100
  46.1 357.1 %all-reduce.2.cloned.1.call-start = ((), (), s32[]{:S(2)}) async-start(), calls=%async_computation.5 | async-start | bytes 524288 | tf_op jit(solution)/shard_map/pmax | solution.py:72
  342.3 129.9 %reduce-scatter.5.cloned.1.call-start = ((), (), s32[]{:S(2)}) async-start(), calls=%async_computation.7 | async-start | bytes 294912 | tf_op jit(solution)/shard_map/reduce_scatter | solution.py:78
  403.1 16.3 %copy-start = (f32[8,32,256]{2,1,0:T(8,128)S(1)}, f32[8,32,256]{2,1,0:T(8,128)}, u32[]{:S(2)}) copy-start(f32[8,32,256]{2,1,0:T(8,128)} %all-reduce.2.cloned.1.call-done) | copy-start | bytes 786436
  419.3 143.8 %reduce-scatter.3.cloned.1.call-start = ((), (), s32[]{:S(2)}) async-start(), calls=%async_computation.6 | async-start | bytes 18874368 | tf_op jit(solution)/shard_map/reduce_scatter | solution.py:77
Sparse Core Ops, SparseCore 0:
  46.2 51.1 all-gather.1
  342.4 60.6 all-reduce.1
  419.5 29.5 reduce-scatter.4
  472.3 90.8 reduce-scatter.2
where the time goes:
time: 580 us; the launch traced here: 578 us
  waiting for transfers between devices  351 us (61%)
  local copies, waits for them, and re-layouts  108 us (19%)
  matrix products  67.7 us (12%)
  other arithmetic  17.9 us (3%)
  blocking collectives  15.5 us (3%)
  between operations  13.3 us (2%)
    all_to_all x1, waiting for transfers between devices, fetch_whole(): lax.all_to_all(found, 'pb', split_axis=0, concat_axis=0, tiled=True)  161 us
    reduce_scatter x1, waiting for transfers between devices, body(): lax.psum_scatter(numerators, 'pa', scatter_dimension=0, tiled=True)  90.9 us
    all_gather x1, waiting for transfers between devices, body(): group_queries = lax.all_gather(queries, 'pa', axis=0, tiled=True)  50.8 us
    pmax x1, waiting for transfers between devices, body(): lax.pmax(value, 'pa')  47.7 us
    dot_general x1, matrix products, attend(): jnp.einsum('jthd,jkhd->jhtk', query_block, key_rows, preferred_element_ty...  30.1 us
    reshape x1, local copies, waits for them, and re-layouts, body(): query_block = group_queries.reshape(Q_GRP, TQ, head_count, DH)  24.4 us
    dot_general x1, matrix products, attend(): jnp.einsum('jhtk,jkhd->jthd', exp_scores.astype(jnp.bfloat16), value_rows...  24.1 us
    transpose x1, local copies, waits for them, and re-layouts, attend(): jnp.einsum('jhtk,jkhd->jthd', exp_scores.astype(jnp.bfloat16), value_rows...  17.4 us
  transfers between devices with their start and end apart: 5, of which 4 were waited for; matrix products, arithmetic and copies ran while one was open for 17% of the time, Pallas kernels for 0%

commit v1 on v0

v1 whole, which is shorter than its diff:
```python
import jax
import jax.numpy as jnp
from jax import lax
from jax.experimental import pallas as pl
from jax.experimental.pallas import tpu as pltpu
from jax.sharding import Mesh, PartitionSpec as P

DH = 64
P_SIZE = 64
TQ = 256
NEG = -1e30


def pack_kernel(pa_ref, k_ref, v_ref, out_ref):
    stored = k_ref.shape[0]

    def write(half):
        lo = half * DH
        for i in range(stored):
            key = k_ref[i, :, lo : lo + DH]
            value = v_ref[i, :, lo : lo + DH].astype(jnp.float32).T.astype(jnp.bfloat16)
            out_ref[0, i] = jnp.concatenate([key, value], axis=1)

    odd = lax.rem(pa_ref[0], 2)

    @pl.when(odd == 0)
    def _():
        write(0)

    @pl.when(odd == 1)
    def _():
        write(1)


def pack_heads(corpus_kv, pa, n_pa, n_y):
    stored, tokens, width2 = corpus_kv.shape
    value_block = width2 // 2 // 128
    per_y = n_pa * DH // 128
    return pl.pallas_call(
        pack_kernel,
        grid_spec=pltpu.PrefetchScalarGridSpec(
            num_scalar_prefetch=1,
            grid=(n_y,),
            in_specs=[
                pl.BlockSpec((stored, tokens, 128), lambda y, pa: (0, 0, y * per_y + pa[0] // 2)),
                pl.BlockSpec(
                    (stored, tokens, 128),
                    lambda y, pa: (0, 0, value_block + y * per_y + pa[0] // 2),
                ),
            ],
            out_specs=pl.BlockSpec((1, stored, tokens, 128), lambda y, pa: (y, 0, 0, 0)),
        ),
        out_shape=jax.ShapeDtypeStruct((n_y, stored, tokens, 128), jnp.bfloat16),
        name="pack_heads",
    )(pa, corpus_kv, corpus_kv)


def query_kernel(hidden_ref, gain_ref, weight_ref, out_ref, normed_ref):
    @pl.when(pl.program_id(0) == 0)
    def _():
        widened = hidden_ref[...].astype(jnp.float32)
        factor = lax.rsqrt(jnp.mean(widened * widened, axis=-1, keepdims=True) + 1e-06)
        normed_ref[...] = (widened * factor * gain_ref[...]).astype(jnp.bfloat16)

    product = jnp.dot(normed_ref[...], weight_ref[...], preferred_element_type=jnp.float32)
    out_ref[...] = product.T.astype(jnp.bfloat16)


def project_queries(hidden, gain, weight):
    rows, width = hidden.shape
    tile = 256
    return pl.pallas_call(
        query_kernel,
        grid=(width // tile,),
        in_specs=[
            pl.BlockSpec((rows, width), lambda i: (0, 0)),
            pl.BlockSpec((1, width), lambda i: (0, 0)),
            pl.BlockSpec((width, tile), lambda i: (0, i)),
        ],
        out_specs=pl.BlockSpec((tile, rows), lambda i: (i, 0)),
        out_shape=jax.ShapeDtypeStruct((width, rows), jnp.bfloat16),
        scratch_shapes=[pltpu.VMEM((rows, width), jnp.bfloat16)],
        compiler_params=pltpu.CompilerParams(vmem_limit_bytes=24 * 2**20),
        name="project_queries",
    )(hidden, gain.reshape(1, width), weight)


def attend_kernel(ids_ref, q_ref, kv_ref, out_ref, score_ref, n_pa, slots_dev):
    questions = q_ref.shape[0]
    slots = n_pa * slots_dev
    group = 4
    lane = lax.broadcasted_iota(jnp.int32, (P_SIZE, 2 * DH), 1)
    pad_row = lax.broadcasted_iota(jnp.int32, (DH, TQ), 0)
    pad = jnp.where(pad_row == 0, 1.0, 0.0).astype(jnp.bfloat16)

    def question(i, carry):
        y, j = i // n_pa, lax.rem(i, n_pa)
        count = ids_ref[y * n_pa, n_pa * slots_dev + j]
        queries = jnp.concatenate([q_ref[i], pad], axis=0)

        def passage(s):
            return ids_ref[y * n_pa + s // slots_dev, j * slots_dev + s % slots_dev]

        def run(parts):
            top = None
            for c in range(parts):
                rows = []
                for s in range(c * group, (c + 1) * group):
                    block = kv_ref[passage(s)]
                    bias = jnp.where(s < count, 0.0, NEG).astype(jnp.bfloat16)
                    rows.append(jnp.where(lane < DH, block, bias))
                scores = jnp.dot(
                    jnp.concatenate(rows, axis=0), queries, preferred_element_type=jnp.float32
                )
                score_ref[c] = scores
                highest = jnp.max(scores.reshape(-1, 8, TQ), axis=0)
                top = highest if top is None else jnp.maximum(top, highest)
            top = jnp.max(top, axis=0, keepdims=True)
            total = jnp.zeros((8, TQ), jnp.float32)
            number = jnp.zeros((DH, TQ), jnp.float32)
            for c in range(parts):
                weights = jnp.exp(score_ref[c] - top)
                total = total + jnp.sum(weights.reshape(-1, 8, TQ), axis=0)
                pairs = []
                for s in range(c * group, (c + 1) * group, 2):
                    first = pltpu.roll(kv_ref[passage(s)], DH, 1)
                    pairs.append(jnp.where(lane < DH, first, kv_ref[passage(s + 1)]))
                number = number + jnp.dot(
                    jnp.concatenate(pairs, axis=1),
                    weights.astype(jnp.bfloat16),
                    preferred_element_type=jnp.float32,
                )
            total = jnp.sum(total, axis=0, keepdims=True)
            out_ref[i] = (number / total).astype(jnp.bfloat16)

        needed = (count + group - 1) // group
        for parts in range(1, slots // group + 1):
            pl.when(needed == parts)(lambda parts=parts: run(parts))
        return carry

    lax.fori_loop(0, questions, question, 0)


def attend(ids, queries, kv, n_pa, slots_dev):
    questions = queries.shape[0]
    passages = kv.shape[0]
    return pl.pallas_call(
        lambda *refs: attend_kernel(*refs, n_pa=n_pa, slots_dev=slots_dev),
        grid_spec=pltpu.PrefetchScalarGridSpec(
            num_scalar_prefetch=1,
            grid=(1,),
            in_specs=[
                pl.BlockSpec((questions, DH, TQ), lambda i, ids: (0, 0, 0)),
                pl.BlockSpec((passages, P_SIZE, 2 * DH), lambda i, ids: (0, 0, 0)),
            ],
            out_specs=pl.BlockSpec((questions, DH, TQ), lambda i, ids: (0, 0, 0)),
            scratch_shapes=[pltpu.VMEM((n_pa * slots_dev // 4, 4 * P_SIZE, TQ), jnp.float32)],
        ),
        out_shape=jax.ShapeDtypeStruct((questions, DH, TQ), jnp.bfloat16),
        compiler_params=pltpu.CompilerParams(vmem_limit_bytes=24 * 2**20),
        name="attend",
    )(ids, queries, kv)


def output_kernel(att_ref, weight_ref, out_ref, rows_ref):
    @pl.when(pl.program_id(0) == 0)
    def _():
        for i in range(0, att_ref.shape[0], TQ):
            part = att_ref[i : i + TQ, :].astype(jnp.float32)
            rows_ref[:, i : i + TQ] = part.T.astype(jnp.bfloat16)

    out_ref[...] = jnp.dot(
        rows_ref[...], weight_ref[...], preferred_element_type=jnp.float32
    ).astype(jnp.bfloat16)


def project_output(attended, weight):
    width, rows = attended.shape
    tile = 256
    return pl.pallas_call(
        output_kernel,
        grid=(width // tile,),
        in_specs=[
            pl.BlockSpec((width, rows), lambda i: (0, 0)),
            pl.BlockSpec((width, tile), lambda i: (0, i)),
        ],
        out_specs=pl.BlockSpec((rows, tile), lambda i: (0, i)),
        out_shape=jax.ShapeDtypeStruct((rows, width), jnp.bfloat16),
        scratch_shapes=[pltpu.VMEM((rows, width), jnp.bfloat16)],
        compiler_params=pltpu.CompilerParams(vmem_limit_bytes=24 * 2**20),
        name="project_output",
    )(attended, weight)


def body(hidden_in, norm_gain, query_weight, out_weight, corpus_kv, owner_ids, local_ids, counts):
    n_y, n_pa = lax.axis_size("y"), lax.axis_size("pa")
    plane = ("y", "pa")
    width = hidden_in.shape[1]
    stored = corpus_kv.shape[0]
    slots_dev = owner_ids.shape[3]
    wanted = (owner_ids[..., 0] * stored + local_ids).reshape(-1)
    ids = lax.all_gather(jnp.concatenate([wanted, counts]), plane, axis=0)
    pa = lax.axis_index("pa").astype(jnp.int32).reshape(1)
    packed = pack_heads(corpus_kv, pa, n_pa, n_y)
    n_z = lax.axis_size("z")
    copies = jnp.broadcast_to(packed[None], (n_z,) + packed.shape).reshape((-1,) + packed.shape[1:])
    kv = lax.all_to_all(copies, ("z", "y"), 0, 0, tiled=True).reshape(-1, P_SIZE, 2 * DH)
    queries = project_queries(hidden_in, norm_gain, query_weight)
    queries = queries.reshape(width // DH, DH, TQ)
    queries = lax.all_to_all(queries, plane, 0, 0, tiled=True)
    attended = attend(ids, queries, kv, n_pa, slots_dev)
    attended = lax.all_to_all(attended, plane, 0, 0, tiled=True)
    return project_output(attended.reshape(width, TQ), out_weight)


def solution(mesh):
    split = Mesh(mesh.devices.reshape(4, 4, 8), ("z", "y", "pa"))
    pb = ("z", "y")
    every = ("z", "y", "pa")
    placed = (
        P(every, None),
        P(),
        P(),
        P(),
        P(pb, None, None),
        P(pb, "pa", None, None, None),
        P(pb, "pa", None, None),
        P(pb),
    )
    return jax.shard_map(
        body, mesh=split, in_specs=placed, out_specs=P(every, None), check_vma=False
    )
```

time: 580 us -> 132 us (0.23)
  waiting for transfers between devices: 351 us -> 13.7 us
  local copies, waits for them, and re-layouts: 108 us -> 12.4 us
  matrix products: 67.7 us -> 0 us
  blocking collectives: 15.5 us -> 55.1 us
  Pallas kernels: 0 us -> 35.2 us
  other arithmetic: 17.9 us -> 0.19 us
  between operations: 13.3 us -> 0.76 us
  starting transfers between devices: 5.64 us -> 13.1 us
    all_to_all x1 -> x2, waiting for transfers between devices: 161 us -> 13.7 us  [the longest x1 13.6 us: body(): queries = lax.all_to_all(queries, plane, 0, 0, tiled=True)]
    reduce_scatter x2 -> x0, waiting for transfers between devices: 91 us -> none  [the longest x1 90.9 us: body(): lax.psum_scatter(numerators, 'pa', scatter_dimension=0, tiled=True)]
    dot_general x4 -> x0, matrix products: 67.7 us -> none  [the longest x1 30.1 us: attend(): jnp.einsum('jthd,jkhd->jhtk', query_block, key_rows, preferred_element_ty...]
    reshape x5 -> x1, local copies, waits for them, and re-layouts: 50.9 us -> 0.08 us  [body(): wanted = (owner_ids[..., 0] * stored + local_ids).reshape(-1)]
    all_gather x1 -> x0, waiting for transfers between devices: 50.8 us -> none  [body(): group_queries = lax.all_gather(queries, 'pa', axis=0, tiled=True)]
    pmax x1 -> x0, waiting for transfers between devices: 47.7 us -> none  [body(): lax.pmax(value, 'pa')]
    pallas_call x0 -> x4, Pallas kernels: none -> 35.2 us  [the longest x1 19.1 us: attend(): pl.pallas_call(lambda *refs: attend_kernel(*refs, n_pa=n_pa, slots_dev=sl...]
    unnamed x0 -> x1, blocking collectives: none -> 32.6 us
  transfers between devices with their start and end apart: 5 -> 2, of which waited for: 4 -> 2; matrix products, arithmetic and copies ran while one was open for 17% -> 1% of each run, Pallas kernels for 0% -> 3%
where the time goes in v1:
time: 132 us; the launch traced here: 130 us
  blocking collectives  55.1 us (42%)
  Pallas kernels  35.2 us (27%)
  waiting for transfers between devices  13.7 us (10%)
  starting transfers between devices  13.1 us (10%)
  local copies, waits for them, and re-layouts  12.4 us (9%)
    unnamed x1, blocking collectives  32.6 us
    all_to_all x1, blocking collectives, body(): attended = lax.all_to_all(attended, plane, 0, 0, tiled=True)  22.5 us
    pallas_call x1, Pallas kernels, attend(): pl.pallas_call(lambda *refs: attend_kernel(*refs, n_pa=n_pa, slots_dev=sl...  19.1 us
    all_to_all x1, waiting for transfers between devices, body(): queries = lax.all_to_all(queries, plane, 0, 0, tiled=True)  13.6 us
    unnamed x18, local copies, waits for them, and re-layouts  9.29 us
    all_to_all x1, starting transfers between devices, body(): queries = lax.all_to_all(queries, plane, 0, 0, tiled=True)  7.4 us
    pallas_call x1, Pallas kernels, project_queries(): pl.pallas_call(query_kernel, grid=(width // tile,), in_specs=[pl.BlockSpe...  6.44 us
    pallas_call x1, Pallas kernels, project_output(): pl.pallas_call(output_kernel, grid=(width // tile,), in_specs=[pl.BlockSp...  5.95 us
  transfers between devices with their start and end apart: 2, of which 2 were waited for; matrix products, arithmetic and copies ran while one was open for 1% of the time, Pallas kernels for 3%

profile of v1, /device:TPU:0, one launch (start us, length us, event | category | flops | bytes accessed | tf_op | source)
XLA Modules:
  0.0 130.5 jit_solution(11377451665254142608)
XLA Ops:
  0.0 0.0 copy-start.1
  0.0 3.4 %copy-done.1 = bf16[2048,2048]{1,0:T(8,128)(2,1)S(1)} copy-done((bf16[2048,2048]{1,0:T(8,128)(2,1)S(1)}, bf16[2048,2048]{1,0:T(8,128)(2,1)}, u32[]{:S(2)}) %copy-start.1) | copy-done | bytes 8388632
  3.4 0.0 copy-start.2
  3.4 1.2 copy-done.2
  4.6 0.0 copy-start.3
  4.6 0.7 copy-done.3
  5.3 6.4 %project_queries.1 = bf16[2048,256]{1,0:T(8,128)(2,1)} custom-call(bf16[256,2048]{1,0:T(8,128)(2,1)S(1)} %copy-done.2, f32[1,2048]{1,0:T(1,128)S(1)} %bitcast.12, bf16[2048,2048]{1,0:T(8,128)(2,1)S(1)} %copy-done.1), custom_call_target="tpu_custom_call" | custom-call | tf_op jit(solution)/shard_map/project_queries/pallas_call | solution.py:72
  11.7 7.4 %all-to-all-start = ((bf16[32,64,256]{2,1,0:T(8,128)(2,1)}), bf16[32,64,256]{2,1,0:T(8,128)(2,1)S(1)}, u32[]{:S(2)}, u32[]{:S(2)}) async-start(bf16[32,64,256]{2,1,0:T(8,128)(2,1)} %bitcast.3), calls=%async_computation | async-start | bytes 2097152 | tf_op jit(solution)/shard_map/all_to_all | solution.py:210
  19.2 3.7 %pack_heads.1 = bf16[4,8,64,128]{3,2,1,0:T(8,128)(2,1)} custom-call(s32[1]{0:T(128)} %bitcast.4.pa_ref, bf16[8,64,4096]{2,1,0:T(8,128)(2,1)} %v_ref.1, bf16[8,64,4096]{2,1,0:T(8,128)(2,1)} %v_ref.1), custom_call_target="tpu_custom_call" | custom-call | tf_op jit(solution)/shard_map/pack_heads/pallas_call | solution.py:39
  22.9 0.0 copy-start.5
  22.9 0.0 copy-start.4
  22.9 0.0 copy-start.7
  22.9 0.0 copy-start.6
  22.9 13.6 %all-to-all-done.refs_1_ = bf16[32,64,256]{2,1,0:T(8,128)(2,1)S(1)} async-done(((bf16[32,64,256]{2,1,0:T(8,128)(2,1)}), bf16[32,64,256]{2,1,0:T(8,128)(2,1)S(1)}, u32[]{:S(2)}, u32[]{:S(2)}) %all-to-all-start) | async-done | bytes 1048608 | tf_op jit(solution)/shard_map/all_to_all | solution.py:210
  36.5 2.9 %broadcast_in_dim.2 = bf16[4,4,8,64,128]{4,3,2,1,0:T(8,128)(2,1)} broadcast(bf16[4,8,64,128]{3,2,1,0:T(8,128)(2,1)} %pack_heads.1), dimensions={1,2,3,4} | broadcast | bytes 2621440 | tf_op jit(solution)/shard_map/broadcast_in_dim | solution.py:206
  39.4 5.7 %all-to-all-start.1 = ((bf16[16,8,64,128]{3,2,1,0:T(8,128)(2,1)}), bf16[16,8,64,128]{3,2,1,0:T(8,128)(2,1)S(1)}, u32[]{:S(2)}, u32[]{:S(2)}) async-start(bf16[16,8,64,128]{3,2,1,0:T(8,128)(2,1)} %bitcast.13), calls=%async_computation.1 | async-start | bytes 4194304 | tf_op jit(solution)/shard_map/all_to_all | solution.py:207
  45.1 0.0 copy-done.5
  45.1 0.0 copy-done.4
  45.1 0.1 copy.10
  45.2 0.1 reshape.36
  45.3 0.0 copy-done.7
  45.3 0.6 dynamic-slice
  46.6 0.0 copy-done.6
  46.6 0.2 add_dynamic-update-slice_fusion
  46.8 32.6 %all-reduce = s32[768]{0:T(1024)S(1)} all-reduce(s32[768]{0:T(1024)S(1)} %add_dynamic-update-slice_fusion), channel_id=2, replica_groups=mesh['z'=4,'y'=4,'pa'=8] {'y','pa'}, use_global_device_ids=true, to_apply=%add | all-reduce | flops 768 | bytes 6144
  79.4 0.1 reshape.43.refs_0_
  79.4 0.1 all-to-all-done.1
  79.5 19.1 %attend.1 = bf16[32,64,256]{2,1,0:T(8,128)(2,1)S(1)} custom-call(s32[32,24]{1,0:T(8,128)S(1)} %reshape.43.refs_0_, bf16[32,64,256]{2,1,0:T(8,128)(2,1)S(1)} %all-to-all-done.refs_1_, bf16[128,64,128]{2,1,0:T(8,128)(2,1)S(1)} %bitcast.10), custom_call_target="tpu_custom_call" | custom-call | tf_op jit(solution)/shard_map/attend/pallas_call | solution.py:147
  98.6 22.5 %all_to_all.15 = bf16[32,64,256]{2,1,0:T(8,128)(2,1)S(1)} all-to-all(bf16[32,64,256]{2,1,0:T(8,128)(2,1)S(1)} %attend.1), channel_id=1, replica_groups=mesh['z'=4,'y'=4,'pa'=8] {'y','pa'}, dimensions={0} | all-to-all | bytes 2097152 | tf_op jit(solution)/shard_map/all_to_all | solution.py:212
  121.1 0.0 copy-start
  121.1 3.4 %copy-done = bf16[2048,2048]{1,0:T(8,128)(2,1)S(1)} copy-done((bf16[2048,2048]{1,0:T(8,128)(2,1)S(1)}, bf16[2048,2048]{1,0:T(8,128)(2,1)}, u32[]{:S(2)}) %copy-start) | copy-done | bytes 8388632
  124.5 6.0 %project_output.1 = bf16[256,2048]{1,0:T(8,128)(2,1)} custom-call(bf16[2048,256]{1,0:T(8,128)(2,1)S(1)} %bitcast.11, bf16[2048,2048]{1,0:T(8,128)(2,1)S(1)} %copy-done), custom_call_target="tpu_custom_call" | custom-call | tf_op jit(solution)/shard_map/project_output/pallas_call | solution.py:180
  (3 shorter events, 0.0 us)
Async XLA Ops:
  0.0 3.4 %copy-start.1 = (bf16[2048,2048]{1,0:T(8,128)(2,1)S(1)}, bf16[2048,2048]{1,0:T(8,128)(2,1)}, u32[]{:S(2)}) copy-start(bf16[2048,2048]{1,0:T(8,128)(2,1)} %weight_ref.2) | copy-start | bytes 25165828
  3.4 1.2 copy-start.2
  4.6 0.7 copy-start.3
  11.7 24.7 %all-to-all-start = ((bf16[32,64,256]{2,1,0:T(8,128)(2,1)}), bf16[32,64,256]{2,1,0:T(8,128)(2,1)S(1)}, u32[]{:S(2)}, u32[]{:S(2)}) async-start(bf16[32,64,256]{2,1,0:T(8,128)(2,1)} %bitcast.3), calls=%async_computation | async-start | bytes 2097152 | tf_op jit(solution)/shard_map/all_to_all | solution.py:210
  22.9 22.2 %copy-start.5 = (s32[1,1,8,2,1]{2,4,3,1,0:T(1,128)S(1)}, s32[1,1,8,2,1]{2,4,3,1,0:T(1,128)}, u32[]{:S(2)}) copy-start(s32[1,1,8,2,1]{2,4,3,1,0:T(1,128)} %param.13) | copy-start | bytes 196
  22.9 22.2 %copy-start.4 = (s32[1,1,8,2]{2,3,1,0:T(2,128)S(1)}, s32[1,1,8,2]{2,3,1,0:T(2,128)}, u32[]{:S(2)}) copy-start(s32[1,1,8,2]{2,3,1,0:T(2,128)} %param.14) | copy-start | bytes 196
  22.9 22.4 %copy-start.7 = (u32[128]{0:T(128)S(1)}, u32[128]{0:T(128)}, u32[]{:S(2)}) copy-start(u32[128]{0:T(128)} %constant.12) | copy-start | bytes 1540
  22.9 23.7 %copy-start.6 = (s32[8]{0:T(128)S(1)}, s32[8]{0:T(128)}, u32[]{:S(2)}) copy-start(s32[8]{0:T(128)} %param.15) | copy-start | bytes 100
  39.4 40.1 %all-to-all-start.1 = ((bf16[16,8,64,128]{3,2,1,0:T(8,128)(2,1)}), bf16[16,8,64,128]{3,2,1,0:T(8,128)(2,1)S(1)}, u32[]{:S(2)}, u32[]{:S(2)}) async-start(bf16[16,8,64,128]{3,2,1,0:T(8,128)(2,1)} %bitcast.13), calls=%async_computation.1 | async-start | bytes 4194304 | tf_op jit(solution)/shard_map/all_to_all | solution.py:207
  121.1 3.4 %copy-start = (bf16[2048,2048]{1,0:T(8,128)(2,1)S(1)}, bf16[2048,2048]{1,0:T(8,128)(2,1)}, u32[]{:S(2)}) copy-start(bf16[2048,2048]{1,0:T(8,128)(2,1)} %weight_ref.3) | copy-start | bytes 25165828

commit v2 on v0

v2 whole, which is shorter than its diff:
```python
import functools

import jax
import jax.numpy as jnp
from jax import lax
from jax.experimental import pallas as pl
from jax.experimental.pallas import tpu as pltpu
from jax.sharding import Mesh, PartitionSpec as P

DH = 64
P_SIZE = 64
TQ = 256
NEG = -1e30
EXTRA = 8
GROUP = 4
SIDE = 4
HEAD_AXES = ("zl", "y", "x")
OWNER_AXES = ("zh", "zl", "y")
EVERY = ("zh", "zl", "y", "x", "c")
LIMIT = 60 * 2**20


def whole():
    return pl.BlockSpec(memory_space=pltpu.VMEM)


def anywhere():
    return pl.BlockSpec(memory_space=pl.ANY)


def pack_kernel(corpus_ref, out_ref, key_ref, value_ref, sems, *, n_x):
    x, core = lax.axis_index("x"), lax.axis_index("c")
    n_far, n_near, half = out_ref.shape[:3]
    width = corpus_ref.shape[2] // 2
    copies = []
    for i in range(n_near):
        column = pl.multiple_of((i * n_x + x) // 2 * 128, 128)
        for n, (held, offset) in enumerate(((key_ref, 0), (value_ref, width))):
            copies.append(
                pltpu.make_async_copy(
                    corpus_ref.at[pl.ds(core * half, half), :, pl.ds(column + offset, 128)],
                    held.at[i],
                    sems.at[i, n],
                )
            )
    for copy in copies:
        copy.start()
    odd = lax.rem(x, 2) == 1
    lane = lax.broadcasted_iota(jnp.int32, (P_SIZE, 2 * DH), 1)
    for i in range(n_near):
        copies[2 * i].wait()
        copies[2 * i + 1].wait()
        for s in range(0, half, 2):
            both = value_ref[i, s : s + 2].reshape(2 * P_SIZE, 2 * DH).astype(jnp.float32).T
            mine = jnp.where(odd, both[DH:], both[:DH]).astype(jnp.bfloat16)
            for n, value in enumerate((pltpu.roll(mine, DH, 1), mine)):
                key = key_ref[i, s + n]
                key = jnp.where(odd, pltpu.roll(key, DH, 1), key)
                entry = jnp.where(lane < DH, key, value)
                for far in range(n_far):
                    out_ref[far, i, s + n] = entry


def pack_heads(corpus_kv, n_far, n_near, n_x):
    stored = corpus_kv.shape[0]
    block = (stored // 2, P_SIZE, 2 * DH)
    return pl.pallas_call(
        functools.partial(pack_kernel, n_x=n_x),
        in_specs=[anywhere()],
        out_specs=whole(),
        out_shape=jax.ShapeDtypeStruct((n_far, n_near) + block, jnp.bfloat16),
        scratch_shapes=[
            pltpu.VMEM((n_near,) + block, jnp.bfloat16),
            pltpu.VMEM((n_near,) + block, jnp.bfloat16),
            pltpu.SemaphoreType.DMA((n_near, 2)),
        ],
        compiler_params=pltpu.CompilerParams(vmem_limit_bytes=LIMIT),
        name="pack_heads",
    )(corpus_kv)


def fetch(weight_ref, held_ref, sems, chunk):
    copies = []
    for n in range(weight_ref.shape[0] // chunk):
        rows = pl.ds(n * chunk, chunk)
        copies.append(pltpu.make_async_copy(weight_ref.at[rows, :], held_ref.at[rows, :], sems.at[n]))
        copies[-1].start()
    return copies


def query_kernel(hidden_ref, gain_ref, extra_ref, weight_ref, out_ref, normed_ref, held_ref, sum_ref, sems):
    rows, width = hidden_ref.shape
    copies = fetch(weight_ref, held_ref, sems, TQ)
    for r in range(0, rows, 64):
        widened = hidden_ref[r : r + 64, :].astype(jnp.float32)
        factor = lax.rsqrt(jnp.mean(widened * widened, axis=-1, keepdims=True) + 1e-06)
        normed_ref[r : r + 64, :] = (widened * factor * gain_ref[...]).astype(jnp.bfloat16)
    for h in range(width // DH):
        out_ref[h, DH:, :] = extra_ref[...]
    for n, copy in enumerate(copies):
        copy.wait()
        depth = slice(n * TQ, (n + 1) * TQ)
        for s in range(0, width, TQ):
            columns = slice(s, s + TQ)
            product = jnp.dot(
                normed_ref[:, depth], held_ref[depth, columns], preferred_element_type=jnp.float32
            )
            if n > 0:
                product = product + sum_ref[:, columns]
            if n < len(copies) - 1:
                sum_ref[:, columns] = product
            else:
                turned = product.T.astype(jnp.bfloat16)
                for h in range(TQ // DH):
                    out_ref[s // DH + h, :DH, :] = turned[h * DH : (h + 1) * DH]


def projection_scratch(rows, width):
    return [
        pltpu.VMEM((rows, width), jnp.bfloat16),
        pltpu.VMEM((width, width), jnp.bfloat16),
        pltpu.VMEM((rows, width), jnp.float32),
        pltpu.SemaphoreType.DMA((width // TQ,)),
    ]


def project_queries(hidden, gain, extra, weight):
    rows, width = hidden.shape
    return pl.pallas_call(
        query_kernel,
        in_specs=[whole(), whole(), whole(), anywhere()],
        out_specs=whole(),
        out_shape=jax.ShapeDtypeStruct((width // DH, DH + EXTRA, rows), jnp.bfloat16),
        scratch_shapes=projection_scratch(rows, width),
        compiler_params=pltpu.CompilerParams(vmem_limit_bytes=LIMIT),
        name="project_queries",
    )(hidden, gain.reshape(1, width), extra, weight)


def output_kernel(attended_ref, weight_ref, out_ref, held_ref, sum_ref, sems):
    width = weight_ref.shape[1]
    copies = fetch(weight_ref, held_ref, sems, TQ)
    for n, copy in enumerate(copies):
        depth = slice(n * TQ, (n + 1) * TQ)
        rows = attended_ref[depth, :].astype(jnp.float32).T.astype(jnp.bfloat16)
        copy.wait()
        for s in range(0, width, TQ):
            columns = slice(s, s + TQ)
            product = jnp.dot(rows, held_ref[depth, columns], preferred_element_type=jnp.float32)
            if n > 0:
                product = product + sum_ref[:, columns]
            if n < len(copies) - 1:
                sum_ref[:, columns] = product
            else:
                out_ref[:, columns] = product.astype(jnp.bfloat16)


def project_output(attended, weight):
    width, rows = attended.shape
    return pl.pallas_call(
        output_kernel,
        in_specs=[whole(), anywhere()],
        out_specs=whole(),
        out_shape=jax.ShapeDtypeStruct((rows, width), jnp.bfloat16),
        scratch_shapes=projection_scratch(rows, width)[1:],
        compiler_params=pltpu.CompilerParams(vmem_limit_bytes=LIMIT),
        name="project_output",
    )(attended, weight)


def attend_kernel(ids_ref, q_ref, mine_ref, other_ref, out_ref, kv_ref, order_ref, sems, *score_refs, n_x):
    core = lax.axis_index("c")
    questions = q_ref.shape[0]
    half = mine_ref.shape[0]
    slots = n_x * 4
    most = slots // GROUP
    copies = [
        pltpu.make_async_copy(ref, kv_ref.at[pl.ds(n * half, half)], sems.at[n])
        for n, ref in enumerate((mine_ref, other_ref))
    ]
    for copy in copies:
        copy.start()
    lane = lax.broadcasted_iota(jnp.int32, (P_SIZE, 2 * DH), 1)
    pad_row = lax.broadcasted_iota(jnp.int32, (DH, TQ), 0)
    pad = jnp.where(pad_row == 0, 1.0, 0.0).astype(jnp.bfloat16)

    def number_in_group(i):
        return lax.rem(i, n_x) * 2 + core

    def count_of(i):
        return ids_ref[i, n_x * 8 + number_in_group(i)]

    def parts_of(i):
        return (count_of(i) + GROUP - 1) // GROUP

    def passage(i, s):
        return ids_ref[
            i // n_x * n_x + s // 4, s // 2 % 2 * n_x * 4 + number_in_group(i) * 2 + s % 2
        ]

    def place(i, at, want):
        order_ref[at] = i
        return at + (parts_of(i) == want).astype(jnp.int32)

    at = jnp.int32(0)
    for want in range(1, most + 1):
        at = lax.fori_loop(0, questions, functools.partial(place, want=want), at)
    for copy in copies:
        copy.wait()

    def run(parts, first):
        chosen = [order_ref[first + g] for g in range(SIDE)]
        tops = []
        for g, i in enumerate(chosen):
            count = count_of(i)
            queries = jnp.concatenate([q_ref[i, :DH, :], pad], axis=0)
            top = None
            for c in range(parts):
                rows = []
                for s in range(c * GROUP, (c + 1) * GROUP):
                    bias = jnp.where(s < count, 0.0, NEG).astype(jnp.bfloat16)
                    rows.append(jnp.where(lane < DH, kv_ref[passage(i, s)], bias))
                scores = jnp.dot(
                    jnp.concatenate(rows, axis=0), queries, preferred_element_type=jnp.float32
                )
                score_refs[g][c] = scores
                highest = jnp.max(scores.reshape(-1, 8, TQ), axis=0)
                top = highest if top is None else jnp.maximum(top, highest)
            tops.append(jnp.max(top, axis=0, keepdims=True))
        for g, i in enumerate(chosen):
            total = jnp.zeros((8, TQ), jnp.float32)
            number = jnp.zeros((DH, TQ), jnp.float32)
            for c in range(parts):
                weights = jnp.exp(score_refs[g][c] - tops[g])
                total = total + jnp.sum(weights.reshape(-1, 8, TQ), axis=0)
                pairs = []
                for s in range(c * GROUP, (c + 1) * GROUP, 2):
                    one = pltpu.roll(kv_ref[passage(i, s)], DH, 1)
                    pairs.append(jnp.where(lane < DH, one, kv_ref[passage(i, s + 1)]))
                number = number + jnp.dot(
                    jnp.concatenate(pairs, axis=1),
                    weights.astype(jnp.bfloat16),
                    preferred_element_type=jnp.float32,
                )
            total = jnp.sum(total, axis=0, keepdims=True)
            out_ref[i] = (number / total).astype(jnp.bfloat16)

    def several(t, carry):
        first = t * SIDE
        needed = parts_of(order_ref[first + SIDE - 1])
        for parts in range(1, most + 1):
            pl.when(needed == parts)(functools.partial(run, parts, first))
        return carry

    lax.fori_loop(0, questions // SIDE, several, 0)


def attend(ids, queries, mine, other, n_x):
    questions = queries.shape[0]
    half = mine.shape[0]
    return pl.pallas_call(
        functools.partial(attend_kernel, n_x=n_x),
        in_specs=[pl.BlockSpec(memory_space=pltpu.SMEM), whole(), anywhere(), anywhere()],
        out_specs=whole(),
        out_shape=jax.ShapeDtypeStruct((questions, DH, TQ), jnp.bfloat16),
        scratch_shapes=[
            pltpu.VMEM((2 * half, P_SIZE, 2 * DH), jnp.bfloat16),
            pltpu.SMEM((questions + 1,), jnp.int32),
            pltpu.SemaphoreType.DMA((2,)),
        ]
        + [pltpu.VMEM((n_x * 4 // GROUP, GROUP * P_SIZE, TQ), jnp.float32)] * SIDE,
        compiler_params=pltpu.CompilerParams(vmem_limit_bytes=LIMIT),
        name="attend",
    )(ids, queries, mine, other)


def swap_cores(value):
    return lax.ppermute(value, "c", [(0, 1), (1, 0)])


def body(hidden_in, norm_gain, query_weight, out_weight, corpus_kv, owner_ids, local_ids, counts):
    n_far, n_near, n_x = lax.axis_size("zh"), lax.axis_size("zl") * lax.axis_size("y"), lax.axis_size("x")
    core = lax.axis_index("c")
    width = hidden_in.shape[1]
    stored = corpus_kv.shape[0]
    wanted = (owner_ids[..., 0] * stored + local_ids).reshape(-1)
    swapped = swap_cores(wanted)
    first, second = jnp.where(core == 0, wanted, swapped), jnp.where(core == 0, swapped, wanted)
    table = jnp.concatenate([first, second, counts]).astype(jnp.bfloat16)
    entries = table.shape[0]
    extra = jnp.broadcast_to(jnp.pad(table, (0, TQ - entries))[None], (EXTRA, TQ))

    packed = pack_heads(corpus_kv, n_far, n_near, n_x)
    packed = packed.reshape((n_far * n_near,) + packed.shape[2:])
    mine = lax.all_to_all(packed, OWNER_AXES, 0, 0, tiled=True).reshape(-1, P_SIZE, 2 * DH)
    other = swap_cores(mine)

    queries = project_queries(hidden_in, norm_gain, extra, query_weight)
    queries = lax.all_to_all(queries, HEAD_AXES, 0, 0, tiled=True)
    ids = queries[:, DH, :entries].astype(jnp.int32)
    half = stored // 2
    local = ids % stored
    place = (local // half ^ core) * (mine.shape[0]) + ids // stored * half + local % half
    ids = jnp.where(jnp.arange(entries)[None, :] < 2 * wanted.shape[0], place, ids)

    attended = attend(ids, queries, mine, other, n_x)
    attended = lax.all_to_all(attended, HEAD_AXES, 0, 0, tiled=True)
    return project_output(attended.reshape(width, TQ), out_weight)


def solution(mesh):
    split = Mesh(mesh.devices.reshape(2, 2, 4, 4, 2), EVERY)
    owner, inner = OWNER_AXES, ("x", "c")
    placed = (
        P(EVERY, None),
        P(),
        P(),
        P(),
        P(owner, None, None),
        P(owner, inner, None, None, None),
        P(owner, inner, None, None),
        P(owner),
    )
    return jax.shard_map(
        body, mesh=split, in_specs=placed, out_specs=P(EVERY, None), check_vma=False
    )
```

time: 580 us -> 94.6 us (0.16)
  waiting for transfers between devices: 351 us -> 28.4 us
  local copies, waits for them, and re-layouts: 108 us -> 2.04 us
  matrix products: 67.7 us -> 0 us
  Pallas kernels: 0 us -> 28.6 us
  other arithmetic: 17.9 us -> 0.85 us
  between operations: 13.3 us -> 0.13 us
  starting transfers between devices: 5.64 us -> 13 us
  blocking collectives: 15.5 us -> 21.6 us
    all_to_all x1 -> x2, waiting for transfers between devices: 161 us -> 27.3 us  [the longest x1 18.1 us: body(): queries = lax.all_to_all(queries, HEAD_AXES, 0, 0, tiled=True)]
    reduce_scatter x2 -> x0, waiting for transfers between devices: 91 us -> none  [the longest x1 90.9 us: body(): lax.psum_scatter(numerators, 'pa', scatter_dimension=0, tiled=True)]
    dot_general x4 -> x0, matrix products: 67.7 us -> none  [the longest x1 30.1 us: attend(): jnp.einsum('jthd,jkhd->jhtk', query_block, key_rows, preferred_element_ty...]
    reshape x5 -> x1, local copies, waits for them, and re-layouts: 50.9 us -> 0.08 us  [body(): wanted = (owner_ids[..., 0] * stored + local_ids).reshape(-1)]
    all_gather x1 -> x0, waiting for transfers between devices: 50.8 us -> none  [body(): group_queries = lax.all_gather(queries, 'pa', axis=0, tiled=True)]
    pmax x1 -> x0, waiting for transfers between devices: 47.7 us -> none  [body(): lax.pmax(value, 'pa')]
    pallas_call x0 -> x4, Pallas kernels: none -> 28.6 us  [the longest x1 12.6 us: attend(): pl.pallas_call(functools.partial(attend_kernel, n_x=n_x), in_specs=[pl.Bl...]
    gather x2 -> x0, local copies, waits for them, and re-layouts: 19.8 us -> none  [the longest x1 10.5 us: fetch_whole(): replies.reshape(group_count * capacity, P_SIZE, 2 * model_width)[target]]
  transfers between devices with their start and end apart: 5 -> 4, of which waited for: 4 -> 3; matrix products, arithmetic and copies ran while one was open for 17% -> 2% of each run, Pallas kernels for 0% -> 7%
where the time goes in v2:
time: 94.6 us; the launch traced here: 94.7 us
  Pallas kernels  28.6 us (30%)
  waiting for transfers between devices  28.4 us (30%)
  blocking collectives  21.6 us (23%)
  starting transfers between devices  13 us (14%)
  local copies, waits for them, and re-layouts  2.04 us (2%)
    all_to_all x1, blocking collectives, body(): attended = lax.all_to_all(attended, HEAD_AXES, 0, 0, tiled=True)  21.6 us
    all_to_all x1, waiting for transfers between devices, body(): queries = lax.all_to_all(queries, HEAD_AXES, 0, 0, tiled=True)  18.1 us
    pallas_call x1, Pallas kernels, attend(): pl.pallas_call(functools.partial(attend_kernel, n_x=n_x), in_specs=[pl.Bl...  12.6 us
    all_to_all x1, waiting for transfers between devices, body(): lax.all_to_all(packed, OWNER_AXES, 0, 0, tiled=True)  9.22 us
    all_to_all x1, starting transfers between devices, body(): lax.all_to_all(packed, OWNER_AXES, 0, 0, tiled=True)  8.14 us
    pallas_call x1, Pallas kernels, project_queries(): pl.pallas_call(query_kernel, in_specs=[whole(), whole(), whole(), anywher...  6.38 us
    pallas_call x1, Pallas kernels, project_output(): pl.pallas_call(output_kernel, in_specs=[whole(), anywhere()], out_specs=w...  6.19 us
    all_to_all x1, starting transfers between devices, body(): queries = lax.all_to_all(queries, HEAD_AXES, 0, 0, tiled=True)  4.79 us
  transfers between devices with their start and end apart: 4, of which 3 were waited for; matrix products, arithmetic and copies ran while one was open for 2% of the time, Pallas kernels for 7%

profile of v2, /device:TPU:0, one launch (start us, length us, event | category | flops | bytes accessed | tf_op | source)
XLA Modules:
  0.0 94.7 jit_solution(5515016782373537188)
XLA Ops:
  0.0 0.0 copy-start.4
  0.0 0.0 copy-start.3
  0.0 0.0 copy-start.5
  0.0 3.5 %pack_heads.1 = bf16[2,8,4,64,128]{4,3,2,1,0:T(8,128)(2,1)} custom-call(bf16[8,64,4096]{2,1,0:T(8,128)(2,1)} %corpus_ref.1), custom_call_target="tpu_custom_call" | custom-call | tf_op jit(solution)/shard_map/pack_heads/pallas_call | solution.py:67
  3.5 8.1 %all-to-all-start.1 = ((bf16[16,4,64,128]{3,2,1,0:T(8,128)(2,1)}), bf16[16,4,64,128]{3,2,1,0:T(8,128)(2,1)S(1)}, u32[]{:S(2)}, u32[]{:S(2)}) async-start(bf16[16,4,64,128]{3,2,1,0:T(8,128)(2,1)} %bitcast.8), calls=%async_computation.1 | async-start | bytes 2097152 | tf_op jit(solution)/shard_map/all_to_all | solution.py:295
  11.6 0.0 copy-done.4
  11.6 0.0 copy-done.3
  11.7 0.1 copy.10
  11.8 0.1 reshape.38
  11.8 0.0 collective-permute-start
  11.9 0.0 copy-done.5
  11.9 1.1 %collective-permute-done = s32[16]{0:T(128)S(1)} collective-permute-done((s32[16]{0:T(128)S(1)}, s32[16]{0:T(128)S(1)}, u32[]{:S(2)}, u32[]{:S(2)}) %collective-permute-start) | collective-permute-done | bytes 96 | tf_op jit(solution)/shard_map/ppermute | solution.py:278
  13.0 0.1 fusion.18
  13.1 0.6 broadcast_in_dim.16.extra_ref
  13.7 6.4 %project_queries.1 = bf16[32,72,256]{2,1,0:T(8,128)(2,1)} custom-call(bf16[256,2048]{1,0:T(8,128)(2,1)} %hidden_ref.1, f32[1,2048]{1,0:T(1,128)} %bitcast.13, bf16[8,256]{1,0:T(8,128)(2,1)} %broadcast_in_dim.16.extra_ref, bf16[2048,2048]{1,0:T(8,128)(2,1)} %weight_ref.2), custom_call_target="tpu_custom_call" | custom-call | tf_op jit(solution)/shard_map/project_queries/pallas_call | solution.py:129
  20.1 9.2 %all-to-all-done.1 = bf16[16,4,64,128]{3,2,1,0:T(8,128)(2,1)S(1)} async-done(((bf16[16,4,64,128]{3,2,1,0:T(8,128)(2,1)}), bf16[16,4,64,128]{3,2,1,0:T(8,128)(2,1)S(1)}, u32[]{:S(2)}, u32[]{:S(2)}) %all-to-all-start.1) | async-done | bytes 1048608 | tf_op jit(solution)/shard_map/all_to_all | solution.py:295
  29.3 0.0 copy-start.1
  29.3 4.8 %all-to-all-start = ((bf16[32,72,256]{2,1,0:T(8,128)(2,1)}), bf16[32,72,256]{2,1,0:T(8,128)(2,1)S(1)}, u32[]{:S(2)}, u32[]{:S(2)}) async-start(bf16[32,72,256]{2,1,0:T(8,128)(2,1)} %project_queries.1), calls=%async_computation | async-start | bytes 2359296 | tf_op jit(solution)/shard_map/all_to_all | solution.py:299
  34.1 0.1 collective-permute-start.1
  34.2 18.1 %all-to-all-done.q_ref = bf16[32,72,256]{2,1,0:T(8,128)(2,1)S(1)} async-done(((bf16[32,72,256]{2,1,0:T(8,128)(2,1)}), bf16[32,72,256]{2,1,0:T(8,128)(2,1)S(1)}, u32[]{:S(2)}, u32[]{:S(2)}) %all-to-all-start) | async-done | bytes 1179680 | tf_op jit(solution)/shard_map/all_to_all | solution.py:299
  52.2 0.0 copy-start
  52.3 0.7 fusion.4.ids_ref
  53.0 0.0 collective-permute-done.1.other_ref
  53.0 0.0 copy-done.1
  53.0 0.3 copy-done
  53.3 0.0 copy-start.2
  53.3 1.0 %copy-done.2 = bf16[64,64,128]{2,1,0:T(8,128)(2,1)} copy-done((bf16[64,64,128]{2,1,0:T(8,128)(2,1)}, bf16[64,64,128]{2,1,0:T(8,128)(2,1)S(1)}, u32[]{:S(2)}) %copy-start.2) | copy-done | bytes 1048600
  54.2 12.6 %attend.1 = bf16[32,64,256]{2,1,0:T(8,128)(2,1)} custom-call(s32[32,40]{1,0:T(8,128)} %fusion.4.ids_ref, bf16[32,72,256]{2,1,0:T(8,128)(2,1)} %copy-done, bf16[64,64,128]{2,1,0:T(8,128)(2,1)} %bitcast.11, bf16[64,64,128]{2,1,0:T(8,128)(2,1)} %copy-done.2), custom_call_target="tpu_custom_call" | custom-call | tf_op jit(solution)/shard_map/attend/pallas_call | solution.py:261
  66.8 21.6 %all_to_all.15 = bf16[32,64,256]{2,1,0:T(8,128)(2,1)} all-to-all(bf16[32,64,256]{2,1,0:T(8,128)(2,1)} %attend.1), channel_id=1, replica_groups=mesh['zh'=2,'zl'=2,'y'=4,'x'=4,'c'=2] {'zl','y','x'}, dimensions={0} | all-to-all | bytes 2097152 | tf_op jit(solution)/shard_map/all_to_all | solution.py:307
  88.5 6.2 %project_output.1 = bf16[256,2048]{1,0:T(8,128)(2,1)} custom-call(bf16[2048,256]{1,0:T(8,128)(2,1)} %bitcast.9, bf16[2048,2048]{1,0:T(8,128)(2,1)} %weight_ref.3), custom_call_target="tpu_custom_call" | custom-call | tf_op jit(solution)/shard_map/project_output/pallas_call | solution.py:160
  (6 shorter events, 0.0 us)
Async XLA Ops:
  0.0 11.6 %copy-start.4 = (s32[1,1,8,2,1]{2,4,3,1,0:T(1,128)S(1)}, s32[1,1,8,2,1]{2,4,3,1,0:T(1,128)}, u32[]{:S(2)}) copy-start(s32[1,1,8,2,1]{2,4,3,1,0:T(1,128)} %param.13) | copy-start | bytes 196
  0.0 11.6 %copy-start.3 = (s32[1,1,8,2]{2,3,1,0:T(2,128)S(1)}, s32[1,1,8,2]{2,3,1,0:T(2,128)}, u32[]{:S(2)}) copy-start(s32[1,1,8,2]{2,3,1,0:T(2,128)} %param.14) | copy-start | bytes 196
  0.0 11.9 %copy-start.5 = (s32[8]{0:T(128)S(1)}, s32[8]{0:T(128)}, u32[]{:S(2)}) copy-start(s32[8]{0:T(128)} %param.15) | copy-start | bytes 100
  3.5 25.8 %all-to-all-start.1 = ((bf16[16,4,64,128]{3,2,1,0:T(8,128)(2,1)}), bf16[16,4,64,128]{3,2,1,0:T(8,128)(2,1)S(1)}, u32[]{:S(2)}, u32[]{:S(2)}) async-start(bf16[16,4,64,128]{3,2,1,0:T(8,128)(2,1)} %bitcast.8), calls=%async_computation.1 | async-start | bytes 2097152 | tf_op jit(solution)/shard_map/all_to_all | solution.py:295
  11.8 1.1 %collective-permute-start = (s32[16]{0:T(128)S(1)}, s32[16]{0:T(128)S(1)}, u32[]{:S(2)}, u32[]{:S(2)}) collective-permute-start(s32[16]{0:T(128)S(1)} %reshape.38), channel_id=1, source_target_pairs={{0,1},{1,0},{2,3},{3,2},{4,5},{5,4},{6,7},{7,6},{8,9},{9,8},{10,11... | collective-permute-start | bytes 200 | tf_op jit(solution)/shard_map/ppermute | solution.py:278
  29.3 23.7 %copy-start.1 = (bf16[16,4,64,128]{3,2,1,0:T(8,128)(2,1)}, bf16[16,4,64,128]{3,2,1,0:T(8,128)(2,1)S(1)}, u32[]{:S(2)}) copy-start(bf16[16,4,64,128]{3,2,1,0:T(8,128)(2,1)S(1)} %all-to-all-done.1) | copy-start | bytes 3145732
  29.3 23.0 %all-to-all-start = ((bf16[32,72,256]{2,1,0:T(8,128)(2,1)}), bf16[32,72,256]{2,1,0:T(8,128)(2,1)S(1)}, u32[]{:S(2)}, u32[]{:S(2)}) async-start(bf16[32,72,256]{2,1,0:T(8,128)(2,1)} %project_queries.1), calls=%async_computation | async-start | bytes 2359296 | tf_op jit(solution)/shard_map/all_to_all | solution.py:299
  34.1 18.9 %collective-permute-start.1 = (bf16[64,64,128]{2,1,0:T(8,128)(2,1)S(1)}, bf16[64,64,128]{2,1,0:T(8,128)(2,1)S(1)}, u32[]{:S(2)}, u32[]{:S(2)}) collective-permute-start(bf16[64,64,128]{2,1,0:T(8,128)(2,1)S(1)} %bitcast.10), channel_id=1, source_target_pairs={{0,1},{1,0},{2,3},{3,2},{4,5},{5,4},{6,7},{7,6},{8,9},{9,8},{10,11... | collective-permute-start | bytes 3145736 | tf_op jit(solution)/shard_map/ppermute | solution.py:278
  52.2 1.0 %copy-start = (bf16[32,72,256]{2,1,0:T(8,128)(2,1)}, bf16[32,72,256]{2,1,0:T(8,128)(2,1)S(1)}, u32[]{:S(2)}) copy-start(bf16[32,72,256]{2,1,0:T(8,128)(2,1)S(1)} %all-to-all-done.q_ref) | copy-start | bytes 3538948
  53.3 1.0 %copy-start.2 = (bf16[64,64,128]{2,1,0:T(8,128)(2,1)}, bf16[64,64,128]{2,1,0:T(8,128)(2,1)S(1)}, u32[]{:S(2)}) copy-start(bf16[64,64,128]{2,1,0:T(8,128)(2,1)S(1)} %collective-permute-done.1.other_ref) | copy-start | bytes 3145732

commit v3 on v2

--- a/solution.py
+++ b/solution.py
@@ -15,6 +15,7 @@
 GROUP = 4
 SIDE = 4
 HEAD_AXES = ("zl", "y", "x")
+NEAR_AXES = ("zl", "y")
 OWNER_AXES = ("zh", "zl", "y")
 EVERY = ("zh", "zl", "y", "x", "c")
 LIMIT = 60 * 2**20
@@ -28,13 +29,17 @@
     return pl.BlockSpec(memory_space=pl.ANY)
 
 
+def turned(i, count, far):
+    return lax.rem(i + count // 2 * far, count)
+
+
 def pack_kernel(corpus_ref, out_ref, key_ref, value_ref, sems, *, n_x):
-    x, core = lax.axis_index("x"), lax.axis_index("c")
-    n_far, n_near, half = out_ref.shape[:3]
+    x, core, far = lax.axis_index("x"), lax.axis_index("c"), lax.axis_index("zh")
+    n_near, half = out_ref.shape[:2]
     width = corpus_ref.shape[2] // 2
     copies = []
     for i in range(n_near):
-        column = pl.multiple_of((i * n_x + x) // 2 * 128, 128)
+        column = pl.multiple_of((turned(i, n_near, far) * n_x + x) // 2 * 128, 128)
         for n, (held, offset) in enumerate(((key_ref, 0), (value_ref, width))):
             copies.append(
                 pltpu.make_async_copy(
@@ -56,19 +61,17 @@
             for n, value in enumerate((pltpu.roll(mine, DH, 1), mine)):
                 key = key_ref[i, s + n]
                 key = jnp.where(odd, pltpu.roll(key, DH, 1), key)
-                entry = jnp.where(lane < DH, key, value)
-                for far in range(n_far):
-                    out_ref[far, i, s + n] = entry
-
-
-def pack_heads(corpus_kv, n_far, n_near, n_x):
+                out_ref[i, s + n] = jnp.where(lane < DH, key, value)
+
+
+def pack_heads(corpus_kv, n_near, n_x):
     stored = corpus_kv.shape[0]
     block = (stored // 2, P_SIZE, 2 * DH)
     return pl.pallas_call(
         functools.partial(pack_kernel, n_x=n_x),
         in_specs=[anywhere()],
         out_specs=whole(),
-        out_shape=jax.ShapeDtypeStruct((n_far, n_near) + block, jnp.bfloat16),
+        out_shape=jax.ShapeDtypeStruct((n_near,) + block, jnp.bfloat16),
         scratch_shapes=[
             pltpu.VMEM((n_near,) + block, jnp.bfloat16),
             pltpu.VMEM((n_near,) + block, jnp.bfloat16),
@@ -79,18 +82,23 @@
     )(corpus_kv)
 
 
-def fetch(weight_ref, held_ref, sems, chunk):
+def fetch(weight_ref, held_ref, sems, chunk_of):
     copies = []
-    for n in range(weight_ref.shape[0] // chunk):
-        rows = pl.ds(n * chunk, chunk)
-        copies.append(pltpu.make_async_copy(weight_ref.at[rows, :], held_ref.at[rows, :], sems.at[n]))
+    for n in range(weight_ref.shape[0] // TQ):
+        rows = pl.ds(pl.multiple_of(chunk_of(n) * TQ, TQ), TQ)
+        copies.append(
+            pltpu.make_async_copy(
+                weight_ref.at[rows, :], held_ref.at[pl.ds(n * TQ, TQ), :], sems.at[n]
+            )
+        )
         copies[-1].start()
     return copies
 
 
 def query_kernel(hidden_ref, gain_ref, extra_ref, weight_ref, out_ref, normed_ref, held_ref, sum_ref, sems):
     rows, width = hidden_ref.shape
-    copies = fetch(weight_ref, held_ref, sems, TQ)
+    far = lax.axis_index("zh")
+    copies = fetch(weight_ref, held_ref, sems, lambda n: n)
     for r in range(0, rows, 64):
         widened = hidden_ref[r : r + 64, :].astype(jnp.float32)
         factor = lax.rsqrt(jnp.mean(widened * widened, axis=-1, keepdims=True) + 1e-06)
@@ -110,9 +118,10 @@
             if n < len(copies) - 1:
                 sum_ref[:, columns] = product
             else:
-                turned = product.T.astype(jnp.bfloat16)
+                by_head = product.T.astype(jnp.bfloat16)
                 for h in range(TQ // DH):
-                    out_ref[s // DH + h, :DH, :] = turned[h * DH : (h + 1) * DH]
+                    place = turned(s // DH + h, width // DH, far)
+                    out_ref[place, :DH, :] = by_head[h * DH : (h + 1) * DH]
 
 
 def projection_scratch(rows, width):
@@ -139,7 +148,8 @@
 
 def output_kernel(attended_ref, weight_ref, out_ref, held_ref, sum_ref, sems):
     width = weight_ref.shape[1]
-    copies = fetch(weight_ref, held_ref, sems, TQ)
+    far = lax.axis_index("zh")
+    copies = fetch(weight_ref, held_ref, sems, lambda n: turned(n, width // TQ, far))
     for n, copy in enumerate(copies):
         depth = slice(n * TQ, (n + 1) * TQ)
         rows = attended_ref[depth, :].astype(jnp.float32).T.astype(jnp.bfloat16)
@@ -168,15 +178,16 @@
     )(attended, weight)
 
 
-def attend_kernel(ids_ref, q_ref, mine_ref, other_ref, out_ref, kv_ref, order_ref, sems, *score_refs, n_x):
+def attend_kernel(ids_ref, q_ref, *refs, n_x):
+    part_refs, (out_ref, kv_ref, order_ref, sems), score_refs = refs[:4], refs[4:8], refs[8:]
     core = lax.axis_index("c")
     questions = q_ref.shape[0]
-    half = mine_ref.shape[0]
+    size = part_refs[0].shape[0]
     slots = n_x * 4
     most = slots // GROUP
     copies = [
-        pltpu.make_async_copy(ref, kv_ref.at[pl.ds(n * half, half)], sems.at[n])
-        for n, ref in enumerate((mine_ref, other_ref))
+        pltpu.make_async_copy(ref, kv_ref.at[pl.ds(n * size, size)], sems.at[n])
+        for n, ref in enumerate(part_refs)
     ]
     for copy in copies:
         copy.start()
@@ -255,23 +266,23 @@
     lax.fori_loop(0, questions // SIDE, several, 0)
 
 
-def attend(ids, queries, mine, other, n_x):
+def attend(ids, queries, parts, n_x):
     questions = queries.shape[0]
-    half = mine.shape[0]
+    size = parts[0].shape[0]
     return pl.pallas_call(
         functools.partial(attend_kernel, n_x=n_x),
-        in_specs=[pl.BlockSpec(memory_space=pltpu.SMEM), whole(), anywhere(), anywhere()],
+        in_specs=[pl.BlockSpec(memory_space=pltpu.SMEM), whole()] + [whole()] * len(parts),
         out_specs=whole(),
         out_shape=jax.ShapeDtypeStruct((questions, DH, TQ), jnp.bfloat16),
         scratch_shapes=[
-            pltpu.VMEM((2 * half, P_SIZE, 2 * DH), jnp.bfloat16),
+            pltpu.VMEM((len(parts) * size, P_SIZE, 2 * DH), jnp.bfloat16),
             pltpu.SMEM((questions + 1,), jnp.int32),
-            pltpu.SemaphoreType.DMA((2,)),
+            pltpu.SemaphoreType.DMA((len(parts),)),
         ]
         + [pltpu.VMEM((n_x * 4 // GROUP, GROUP * P_SIZE, TQ), jnp.float32)] * SIDE,
-        compiler_params=pltpu.CompilerParams(vmem_limit_bytes=LIMIT),
+        compiler_params=pltpu.CompilerParams(vmem_limit_bytes=20 * 2**20),
         name="attend",
-    )(ids, queries, mine, other)
+    )(ids, queries, *parts)
 
 
 def swap_cores(value):
@@ -279,8 +290,8 @@
 
 
 def body(hidden_in, norm_gain, query_weight, out_weight, corpus_kv, owner_ids, local_ids, counts):
-    n_far, n_near, n_x = lax.axis_size("zh"), lax.axis_size("zl") * lax.axis_size("y"), lax.axis_size("x")
-    core = lax.axis_index("c")
+    n_near, n_x = lax.axis_size("zl") * lax.axis_size("y"), lax.axis_size("x")
+    far_index, core = lax.axis_index("zh"), lax.axis_index("c")
     width = hidden_in.shape[1]
     stored = corpus_kv.shape[0]
     wanted = (owner_ids[..., 0] * stored + local_ids).reshape(-1)
@@ -290,20 +301,21 @@
     entries = table.shape[0]
     extra = jnp.broadcast_to(jnp.pad(table, (0, TQ - entries))[None], (EXTRA, TQ))
 
-    packed = pack_heads(corpus_kv, n_far, n_near, n_x)
-    packed = packed.reshape((n_far * n_near,) + packed.shape[2:])
-    mine = lax.all_to_all(packed, OWNER_AXES, 0, 0, tiled=True).reshape(-1, P_SIZE, 2 * DH)
-    other = swap_cores(mine)
+    packed = pack_heads(corpus_kv, n_near, n_x)
+    near = lax.all_to_all(packed, NEAR_AXES, 0, 0, tiled=True).reshape(-1, P_SIZE, 2 * DH)
+    far = lax.ppermute(near, ("zh", "zl"), [(0, 3), (3, 0), (1, 2), (2, 1)])
+    parts = (near, swap_cores(near), far, swap_cores(far))
 
     queries = project_queries(hidden_in, norm_gain, extra, query_weight)
     queries = lax.all_to_all(queries, HEAD_AXES, 0, 0, tiled=True)
     ids = queries[:, DH, :entries].astype(jnp.int32)
     half = stored // 2
-    local = ids % stored
-    place = (local // half ^ core) * (mine.shape[0]) + ids // stored * half + local % half
+    owner, local = ids // stored, ids % stored
+    part = (owner // n_near ^ far_index) * 2 + (local // half ^ core)
+    place = (part * n_near + owner % n_near) * half + local % half
     ids = jnp.where(jnp.arange(entries)[None, :] < 2 * wanted.shape[0], place, ids)
 
-    attended = attend(ids, queries, mine, other, n_x)
+    attended = attend(ids, queries, parts, n_x)
     attended = lax.all_to_all(attended, HEAD_AXES, 0, 0, tiled=True)
     return project_output(attended.reshape(width, TQ), out_weight)
 

time: 94.6 us -> 86.4 us (0.913)
  waiting for transfers between devices: 28.4 us -> 17.4 us
  starting transfers between devices: 13 us -> 16.8 us
  blocking collectives: 21.6 us -> 23 us
  local copies, waits for them, and re-layouts: 2.04 us -> 0.77 us
  Pallas kernels: 28.6 us -> 27.5 us
    all_to_all x1, waiting for transfers between devices: 18.1 us -> 2.9 us  [body(): queries = lax.all_to_all(queries, HEAD_AXES, 0, 0, tiled=True)]
    ppermute x0 -> x1, waiting for transfers between devices: none -> 11.7 us  [body(): far = lax.ppermute(near, ('zh', 'zl'), [(0, 3), (3, 0), (1, 2), (2, 1)])]
    all_to_all x1, waiting for transfers between devices: 9.22 us -> 1.67 us  [body(): lax.all_to_all(packed, NEAR_AXES, 0, 0, tiled=True)]
    ppermute x0 -> x1, starting transfers between devices: none -> 4 us  [body(): far = lax.ppermute(near, ('zh', 'zl'), [(0, 3), (3, 0), (1, 2), (2, 1)])]
    all_to_all x1, starting transfers between devices: 8.14 us -> 5.92 us  [body(): lax.all_to_all(packed, NEAR_AXES, 0, 0, tiled=True)]
    all_to_all x1, starting transfers between devices: 4.79 us -> 6.89 us  [body(): queries = lax.all_to_all(queries, HEAD_AXES, 0, 0, tiled=True)]
    all_to_all x1, blocking collectives: 21.6 us -> 23 us  [body(): attended = lax.all_to_all(attended, HEAD_AXES, 0, 0, tiled=True)]
    unnamed x12 -> x6, local copies, waits for them, and re-layouts: 1.27 us -> 0.01 us
  transfers between devices with their start and end apart: 4 -> 6, of which waited for: 3 -> 4; matrix products, arithmetic and copies ran while one was open for 2% -> 1% of each run, Pallas kernels for 7% -> 7%
where the time goes in v3:
time: 86.4 us; the launch traced here: 85.8 us
  Pallas kernels  27.5 us (32%)
  blocking collectives  23 us (27%)
  waiting for transfers between devices  17.4 us (20%)
  starting transfers between devices  16.8 us (19%)
    all_to_all x1, blocking collectives, body(): attended = lax.all_to_all(attended, HEAD_AXES, 0, 0, tiled=True)  23 us
    ppermute x1, waiting for transfers between devices, body(): far = lax.ppermute(near, ('zh', 'zl'), [(0, 3), (3, 0), (1, 2), (2, 1)])  11.7 us
    pallas_call x1, Pallas kernels, attend(): pl.pallas_call(functools.partial(attend_kernel, n_x=n_x), in_specs=[pl.Bl...  11.6 us
    all_to_all x1, starting transfers between devices, body(): queries = lax.all_to_all(queries, HEAD_AXES, 0, 0, tiled=True)  6.89 us
    pallas_call x1, Pallas kernels, project_queries(): pl.pallas_call(query_kernel, in_specs=[whole(), whole(), whole(), anywher...  6.38 us
    pallas_call x1, Pallas kernels, project_output(): pl.pallas_call(output_kernel, in_specs=[whole(), anywhere()], out_specs=w...  6.21 us
    all_to_all x1, starting transfers between devices, body(): lax.all_to_all(packed, NEAR_AXES, 0, 0, tiled=True)  5.92 us
    ppermute x1, starting transfers between devices, body(): far = lax.ppermute(near, ('zh', 'zl'), [(0, 3), (3, 0), (1, 2), (2, 1)])  4 us
  transfers between devices with their start and end apart: 6, of which 4 were waited for; matrix products, arithmetic and copies ran while one was open for 1% of the time, Pallas kernels for 7%

profile of v3, /device:TPU:0, one launch (start us, length us, event | category | flops | bytes accessed | tf_op | source)
XLA Modules:
  0.0 85.8 jit_solution(8330383752890099403)
XLA Ops:
  0.0 0.0 copy-start.1
  0.0 0.0 copy-start
  0.0 0.0 copy-start.2
  0.0 3.3 %pack_heads.1 = bf16[8,4,64,128]{3,2,1,0:T(8,128)(2,1)} custom-call(bf16[8,64,4096]{2,1,0:T(8,128)(2,1)} %corpus_ref.1), custom_call_target="tpu_custom_call" | custom-call | tf_op jit(solution)/shard_map/pack_heads/pallas_call | solution.py:70
  3.3 5.9 %all-to-all-start.1 = ((bf16[8,4,64,128]{3,2,1,0:T(8,128)(2,1)}), bf16[8,4,64,128]{3,2,1,0:T(8,128)(2,1)S(1)}, u32[]{:S(2)}, u32[]{:S(2)}) async-start(bf16[8,4,64,128]{3,2,1,0:T(8,128)(2,1)} %pack_heads.1), calls=%async_computation.1 | async-start | bytes 1048576 | tf_op jit(solution)/shard_map/all_to_all | solution.py:305
  9.2 0.0 copy-done.1
  9.2 0.0 copy-done
  9.3 0.1 copy.10
  9.3 0.1 reshape.35
  9.4 0.0 collective-permute-start
  9.5 0.0 copy-done.2
  9.5 1.1 %collective-permute-done = s32[16]{0:T(128)S(1)} collective-permute-done((s32[16]{0:T(128)S(1)}, s32[16]{0:T(128)S(1)}, u32[]{:S(2)}, u32[]{:S(2)}) %collective-permute-start) | collective-permute-done | bytes 96 | tf_op jit(solution)/shard_map/ppermute | solution.py:289
  10.6 0.1 fusion.25
  10.6 0.6 broadcast_in_dim.16.extra_ref
  11.2 6.4 %project_queries.1 = bf16[32,72,256]{2,1,0:T(8,128)(2,1)} custom-call(bf16[256,2048]{1,0:T(8,128)(2,1)} %hidden_ref.1, f32[1,2048]{1,0:T(1,128)} %bitcast.12, bf16[8,256]{1,0:T(8,128)(2,1)} %broadcast_in_dim.16.extra_ref, bf16[2048,2048]{1,0:T(8,128)(2,1)} %weight_ref.2), custom_call_target="tpu_custom_call" | custom-call | tf_op jit(solution)/shard_map/project_queries/pallas_call | solution.py:138
  17.6 1.7 %all-to-all-done.1 = bf16[8,4,64,128]{3,2,1,0:T(8,128)(2,1)S(1)} async-done(((bf16[8,4,64,128]{3,2,1,0:T(8,128)(2,1)}), bf16[8,4,64,128]{3,2,1,0:T(8,128)(2,1)S(1)}, u32[]{:S(2)}, u32[]{:S(2)}) %all-to-all-start.1) | async-done | bytes 524320 | tf_op jit(solution)/shard_map/all_to_all | solution.py:305
  19.3 6.9 %all-to-all-start = ((bf16[32,72,256]{2,1,0:T(8,128)(2,1)}), bf16[32,72,256]{2,1,0:T(8,128)(2,1)S(1)}, u32[]{:S(2)}, u32[]{:S(2)}) async-start(bf16[32,72,256]{2,1,0:T(8,128)(2,1)} %project_queries.1), calls=%async_computation | async-start | bytes 2359296 | tf_op jit(solution)/shard_map/all_to_all | solution.py:310
  26.2 4.0 %collective-permute-start.2 = (bf16[32,64,128]{2,1,0:T(8,128)(2,1)S(1)}, bf16[32,64,128]{2,1,0:T(8,128)(2,1)S(1)}, u32[]{:S(2)}, u32[]{:S(2)}) collective-permute-start(bf16[32,64,128]{2,1,0:T(8,128)(2,1)S(1)} %bitcast.7), channel_id=1, source_target_pairs={{0,96},{96,0},{32,64},{64,32},{1,97},{97,1},{33,65},{65,33},{2,98}... | collective-permute-start | bytes 1572872 | tf_op jit(solution)/shard_map/ppermute | solution.py:306
  30.2 0.0 collective-permute-start.1
  30.2 11.7 %collective-permute-done.2.refs_2_ = bf16[32,64,128]{2,1,0:T(8,128)(2,1)S(1)} collective-permute-done((bf16[32,64,128]{2,1,0:T(8,128)(2,1)S(1)}, bf16[32,64,128]{2,1,0:T(8,128)(2,1)S(1)}, u32[]{:S(2)}, u32[]{:S(2)}) %collective-permute-start.2) | collective-permute-done | bytes 524320 | tf_op jit(solution)/shard_map/ppermute | solution.py:306
  41.9 0.0 collective-permute-start.3
  41.9 2.9 %all-to-all-done.q_ref = bf16[32,72,256]{2,1,0:T(8,128)(2,1)S(1)} async-done(((bf16[32,72,256]{2,1,0:T(8,128)(2,1)}), bf16[32,72,256]{2,1,0:T(8,128)(2,1)S(1)}, u32[]{:S(2)}, u32[]{:S(2)}) %all-to-all-start) | async-done | bytes 1179680 | tf_op jit(solution)/shard_map/all_to_all | solution.py:310
  44.9 0.1 fusion.7.ids_ref
  44.9 0.0 collective-permute-done.1.refs_1_
  44.9 0.0 collective-permute-done.3.refs_3_
  44.9 11.6 %attend.1 = bf16[32,64,256]{2,1,0:T(8,128)(2,1)S(1)} custom-call(s32[32,40]{1,0:T(8,128)S(1)} %fusion.7.ids_ref, bf16[32,72,256]{2,1,0:T(8,128)(2,1)S(1)} %all-to-all-done.q_ref, bf16[32,64,128]{2,1,0:T(8,128)(2,1)S(1)} %bitcast.9, bf16[32,64,128]{2,1,0:T(8,128)(2,1)S(1)} %collective-permute-done.1.refs_1_, ...), custom_call_target="tpu_custom_call" | custom-call | tf_op jit(solution)/shard_map/attend/pallas_call | solution.py:272
  56.5 23.0 %all_to_all.15 = bf16[32,64,256]{2,1,0:T(8,128)(2,1)} all-to-all(bf16[32,64,256]{2,1,0:T(8,128)(2,1)S(1)} %attend.1), channel_id=1, replica_groups=mesh['zh'=2,'zl'=2,'y'=4,'x'=4,'c'=2] {'zl','y','x'}, dimensions={0} | all-to-all | bytes 2097152 | tf_op jit(solution)/shard_map/all_to_all | solution.py:319
  79.6 6.2 %project_output.1 = bf16[256,2048]{1,0:T(8,128)(2,1)} custom-call(bf16[2048,256]{1,0:T(8,128)(2,1)} %bitcast.10, bf16[2048,2048]{1,0:T(8,128)(2,1)} %weight_ref.3), custom_call_target="tpu_custom_call" | custom-call | tf_op jit(solution)/shard_map/project_output/pallas_call | solution.py:170
  (6 shorter events, 0.0 us)
Async XLA Ops:
  0.0 9.2 %copy-start.1 = (s32[1,1,8,2,1]{2,4,3,1,0:T(1,128)S(1)}, s32[1,1,8,2,1]{2,4,3,1,0:T(1,128)}, u32[]{:S(2)}) copy-start(s32[1,1,8,2,1]{2,4,3,1,0:T(1,128)} %param.13) | copy-start | bytes 196
  0.0 9.2 %copy-start = (s32[1,1,8,2]{2,3,1,0:T(2,128)S(1)}, s32[1,1,8,2]{2,3,1,0:T(2,128)}, u32[]{:S(2)}) copy-start(s32[1,1,8,2]{2,3,1,0:T(2,128)} %param.14) | copy-start | bytes 196
  0.0 9.4 %copy-start.2 = (s32[8]{0:T(128)S(1)}, s32[8]{0:T(128)}, u32[]{:S(2)}) copy-start(s32[8]{0:T(128)} %param.15) | copy-start | bytes 100
  3.3 16.0 %all-to-all-start.1 = ((bf16[8,4,64,128]{3,2,1,0:T(8,128)(2,1)}), bf16[8,4,64,128]{3,2,1,0:T(8,128)(2,1)S(1)}, u32[]{:S(2)}, u32[]{:S(2)}) async-start(bf16[8,4,64,128]{3,2,1,0:T(8,128)(2,1)} %pack_heads.1), calls=%async_computation.1 | async-start | bytes 1048576 | tf_op jit(solution)/shard_map/all_to_all | solution.py:305
  9.4 1.1 %collective-permute-start = (s32[16]{0:T(128)S(1)}, s32[16]{0:T(128)S(1)}, u32[]{:S(2)}, u32[]{:S(2)}) collective-permute-start(s32[16]{0:T(128)S(1)} %reshape.35), channel_id=1, source_target_pairs={{0,1},{1,0},{2,3},{3,2},{4,5},{5,4},{6,7},{7,6},{8,9},{9,8},{10,11... | collective-permute-start | bytes 200 | tf_op jit(solution)/shard_map/ppermute | solution.py:289
  19.3 25.5 %all-to-all-start = ((bf16[32,72,256]{2,1,0:T(8,128)(2,1)}), bf16[32,72,256]{2,1,0:T(8,128)(2,1)S(1)}, u32[]{:S(2)}, u32[]{:S(2)}) async-start(bf16[32,72,256]{2,1,0:T(8,128)(2,1)} %project_queries.1), calls=%async_computation | async-start | bytes 2359296 | tf_op jit(solution)/shard_map/all_to_all | solution.py:310
  26.2 15.7 %collective-permute-start.2 = (bf16[32,64,128]{2,1,0:T(8,128)(2,1)S(1)}, bf16[32,64,128]{2,1,0:T(8,128)(2,1)S(1)}, u32[]{:S(2)}, u32[]{:S(2)}) collective-permute-start(bf16[32,64,128]{2,1,0:T(8,128)(2,1)S(1)} %bitcast.7), channel_id=1, source_target_pairs={{0,96},{96,0},{32,64},{64,32},{1,97},{97,1},{33,65},{65,33},{2,98}... | collective-permute-start | bytes 1572872 | tf_op jit(solution)/shard_map/ppermute | solution.py:306
  30.2 14.7 %collective-permute-start.1 = (bf16[32,64,128]{2,1,0:T(8,128)(2,1)S(1)}, bf16[32,64,128]{2,1,0:T(8,128)(2,1)S(1)}, u32[]{:S(2)}, u32[]{:S(2)}) collective-permute-start(bf16[32,64,128]{2,1,0:T(8,128)(2,1)S(1)} %bitcast.8), channel_id=1, source_target_pairs={{0,1},{1,0},{2,3},{3,2},{4,5},{5,4},{6,7},{7,6},{8,9},{9,8},{10,11... | collective-permute-start | bytes 1572872 | tf_op jit(solution)/shard_map/ppermute | solution.py:289
  41.9 3.0 %collective-permute-start.3 = (bf16[32,64,128]{2,1,0:T(8,128)(2,1)S(1)}, bf16[32,64,128]{2,1,0:T(8,128)(2,1)S(1)}, u32[]{:S(2)}, u32[]{:S(2)}) collective-permute-start(bf16[32,64,128]{2,1,0:T(8,128)(2,1)S(1)} %collective-permute-done.2.refs_2_), channel_id=1, source_target_pairs={{0,1},{1,0},{2,3},{3,2},{4,5},{5,4},{6,7},{7,6},{8,9},{9,8},{10,11... | collective-permute-start | bytes 1572872 | tf_op jit(solution)/shard_map/ppermute | solution.py:289

commit v4 on v3

--- a/solution.py
+++ b/solution.py
@@ -13,7 +13,7 @@
 NEG = -1e30
 EXTRA = 8
 GROUP = 4
-SIDE = 4
+SIDE = 8
 HEAD_AXES = ("zl", "y", "x")
 NEAR_AXES = ("zl", "y")
 OWNER_AXES = ("zh", "zl", "y")
@@ -52,12 +52,12 @@
         copy.start()
     odd = lax.rem(x, 2) == 1
     lane = lax.broadcasted_iota(jnp.int32, (P_SIZE, 2 * DH), 1)
+    for copy in copies:
+        copy.wait()
     for i in range(n_near):
-        copies[2 * i].wait()
-        copies[2 * i + 1].wait()
         for s in range(0, half, 2):
-            both = value_ref[i, s : s + 2].reshape(2 * P_SIZE, 2 * DH).astype(jnp.float32).T
-            mine = jnp.where(odd, both[DH:], both[:DH]).astype(jnp.bfloat16)
+            both = value_ref[i, s : s + 2].reshape(2 * P_SIZE, 2 * DH).T
+            mine = jnp.where(odd, both[DH:], both[:DH])
             for n, value in enumerate((pltpu.roll(mine, DH, 1), mine)):
                 key = key_ref[i, s + n]
                 key = jnp.where(odd, pltpu.roll(key, DH, 1), key)
@@ -146,41 +146,34 @@
     )(hidden, gain.reshape(1, width), extra, weight)
 
 
-def output_kernel(attended_ref, weight_ref, out_ref, held_ref, sum_ref, sems):
+def output_kernel(attended_ref, weight_ref, out_ref, rows_ref):
     width = weight_ref.shape[1]
-    far = lax.axis_index("zh")
-    copies = fetch(weight_ref, held_ref, sems, lambda n: turned(n, width // TQ, far))
-    for n, copy in enumerate(copies):
-        depth = slice(n * TQ, (n + 1) * TQ)
-        rows = attended_ref[depth, :].astype(jnp.float32).T.astype(jnp.bfloat16)
-        copy.wait()
-        for s in range(0, width, TQ):
-            columns = slice(s, s + TQ)
-            product = jnp.dot(rows, held_ref[depth, columns], preferred_element_type=jnp.float32)
-            if n > 0:
-                product = product + sum_ref[:, columns]
-            if n < len(copies) - 1:
-                sum_ref[:, columns] = product
-            else:
-                out_ref[:, columns] = product.astype(jnp.bfloat16)
+    for n in range(0, width, TQ):
+        rows_ref[:, n : n + TQ] = attended_ref[n : n + TQ, :].T
+    for n in range(0, width, TQ):
+        columns = slice(n, n + TQ)
+        out_ref[:, columns] = jnp.dot(
+            rows_ref[...], weight_ref[:, columns], preferred_element_type=jnp.float32
+        ).astype(jnp.bfloat16)
 
 
 def project_output(attended, weight):
     width, rows = attended.shape
     return pl.pallas_call(
         output_kernel,
-        in_specs=[whole(), anywhere()],
+        in_specs=[whole(), whole()],
         out_specs=whole(),
         out_shape=jax.ShapeDtypeStruct((rows, width), jnp.bfloat16),
-        scratch_shapes=projection_scratch(rows, width)[1:],
-        compiler_params=pltpu.CompilerParams(vmem_limit_bytes=LIMIT),
+        scratch_shapes=[pltpu.VMEM((rows, width), jnp.bfloat16)],
+        compiler_params=pltpu.CompilerParams(vmem_limit_bytes=16 * 2**20),
         name="project_output",
-    )(attended, weight)
+    )(attended, pltpu.with_memory_space_constraint(weight, pltpu.VMEM))
 
 
 def attend_kernel(ids_ref, q_ref, *refs, n_x):
-    part_refs, (out_ref, kv_ref, order_ref, sems), score_refs = refs[:4], refs[4:8], refs[8:]
-    core = lax.axis_index("c")
+    part_refs, weight_ref, (out_ref, held_ref), refs = refs[:4], refs[4], refs[5:7], refs[7:]
+    (kv_ref, order_ref, sems, weight_sems), score_refs = refs[:4], refs[4:]
+    core, far = lax.axis_index("c"), lax.axis_index("zh")
     questions = q_ref.shape[0]
     size = part_refs[0].shape[0]
     slots = n_x * 4
@@ -191,12 +184,14 @@
     ]
     for copy in copies:
         copy.start()
+    chunks = weight_ref.shape[0] // TQ
+    weights_in = fetch(weight_ref, held_ref, weight_sems, lambda n: turned(n, chunks, far))
     lane = lax.broadcasted_iota(jnp.int32, (P_SIZE, 2 * DH), 1)
     pad_row = lax.broadcasted_iota(jnp.int32, (DH, TQ), 0)
     pad = jnp.where(pad_row == 0, 1.0, 0.0).astype(jnp.bfloat16)
 
     def number_in_group(i):
-        return lax.rem(i, n_x) * 2 + core
+        return i % n_x * 2 + core
 
     def count_of(i):
         return ids_ref[i, n_x * 8 + number_in_group(i)]
@@ -209,13 +204,12 @@
             i // n_x * n_x + s // 4, s // 2 % 2 * n_x * 4 + number_in_group(i) * 2 + s % 2
         ]
 
-    def place(i, at, want):
-        order_ref[at] = i
-        return at + (parts_of(i) == want).astype(jnp.int32)
-
+    needs = [parts_of(i) for i in range(questions)]
     at = jnp.int32(0)
     for want in range(1, most + 1):
-        at = lax.fori_loop(0, questions, functools.partial(place, want=want), at)
+        for i in range(questions):
+            order_ref[at] = i
+            at = at + jnp.where(needs[i] == want, 1, 0)
     for copy in copies:
         copy.wait()
 
@@ -264,25 +258,31 @@
         return carry
 
     lax.fori_loop(0, questions // SIDE, several, 0)
-
-
-def attend(ids, queries, parts, n_x):
+    for copy in weights_in:
+        copy.wait()
+
+
+def attend(ids, queries, parts, weight, n_x):
     questions = queries.shape[0]
     size = parts[0].shape[0]
     return pl.pallas_call(
         functools.partial(attend_kernel, n_x=n_x),
-        in_specs=[pl.BlockSpec(memory_space=pltpu.SMEM), whole()] + [whole()] * len(parts),
-        out_specs=whole(),
-        out_shape=jax.ShapeDtypeStruct((questions, DH, TQ), jnp.bfloat16),
+        in_specs=[pl.BlockSpec(memory_space=pltpu.SMEM), whole()] + [whole()] * len(parts) + [pl.BlockSpec(memory_space=pltpu.HBM)],
+        out_specs=(whole(), whole()),
+        out_shape=(
+            jax.ShapeDtypeStruct((questions, DH, TQ), jnp.bfloat16),
+            pltpu.VMEM(weight.shape, jnp.bfloat16),
+        ),
         scratch_shapes=[
             pltpu.VMEM((len(parts) * size, P_SIZE, 2 * DH), jnp.bfloat16),
             pltpu.SMEM((questions + 1,), jnp.int32),
             pltpu.SemaphoreType.DMA((len(parts),)),
+            pltpu.SemaphoreType.DMA((weight.shape[0] // TQ,)),
         ]
         + [pltpu.VMEM((n_x * 4 // GROUP, GROUP * P_SIZE, TQ), jnp.float32)] * SIDE,
-        compiler_params=pltpu.CompilerParams(vmem_limit_bytes=20 * 2**20),
+        compiler_params=pltpu.CompilerParams(vmem_limit_bytes=32 * 2**20),
         name="attend",
-    )(ids, queries, *parts)
+    )(ids, queries, *parts, pltpu.with_memory_space_constraint(weight, pltpu.HBM))
 
 
 def swap_cores(value):
@@ -315,9 +315,9 @@
     place = (part * n_near + owner % n_near) * half + local % half
     ids = jnp.where(jnp.arange(entries)[None, :] < 2 * wanted.shape[0], place, ids)
 
-    attended = attend(ids, queries, parts, n_x)
+    attended, weight = attend(ids, queries, parts, out_weight, n_x)
     attended = lax.all_to_all(attended, HEAD_AXES, 0, 0, tiled=True)
-    return project_output(attended.reshape(width, TQ), out_weight)
+    return project_output(attended.reshape(width, TQ), weight)
 
 
 def solution(mesh):

time: 86.4 us -> 79.6 us (0.921)
  Pallas kernels: 27.5 us -> 21.5 us
  blocking collectives: 23 us -> 21.9 us
    pallas_call x1, Pallas kernels: 6.21 us -> 3.33 us  [project_output(): pl.pallas_call(output_kernel, in_specs=[whole(), whole()], out_specs=whol...]
    pallas_call x1, Pallas kernels: 11.6 us -> 9.14 us  [attend(): pl.pallas_call(functools.partial(attend_kernel, n_x=n_x), in_specs=[pl.Bl...]
    all_to_all x1, blocking collectives: 23 us -> 21.9 us  [body(): attended = lax.all_to_all(attended, HEAD_AXES, 0, 0, tiled=True)]
  transfers between devices with their start and end apart: 6 -> 6, of which waited for: 4 -> 4; matrix products, arithmetic and copies ran while one was open for 1% -> 1% of each run, Pallas kernels for 7% -> 8%
where the time goes in v4:
time: 79.6 us; the launch traced here: 78.7 us
  blocking collectives  21.9 us (28%)
  Pallas kernels  21.5 us (27%)
  waiting for transfers between devices  17.4 us (22%)
  starting transfers between devices  16.9 us (21%)
    all_to_all x1, blocking collectives, body(): attended = lax.all_to_all(attended, HEAD_AXES, 0, 0, tiled=True)  21.9 us
    ppermute x1, waiting for transfers between devices, body(): far = lax.ppermute(near, ('zh', 'zl'), [(0, 3), (3, 0), (1, 2), (2, 1)])  11.7 us
    pallas_call x1, Pallas kernels, attend(): pl.pallas_call(functools.partial(attend_kernel, n_x=n_x), in_specs=[pl.Bl...  9.14 us
    all_to_all x1, starting transfers between devices, body(): queries = lax.all_to_all(queries, HEAD_AXES, 0, 0, tiled=True)  6.92 us
    pallas_call x1, Pallas kernels, project_queries(): pl.pallas_call(query_kernel, in_specs=[whole(), whole(), whole(), anywher...  6.39 us
    all_to_all x1, starting transfers between devices, body(): lax.all_to_all(packed, NEAR_AXES, 0, 0, tiled=True)  5.93 us
    ppermute x1, starting transfers between devices, body(): far = lax.ppermute(near, ('zh', 'zl'), [(0, 3), (3, 0), (1, 2), (2, 1)])  4 us
    pallas_call x1, Pallas kernels, project_output(): pl.pallas_call(output_kernel, in_specs=[whole(), whole()], out_specs=whol...  3.33 us
  transfers between devices with their start and end apart: 6, of which 4 were waited for; matrix products, arithmetic and copies ran while one was open for 1% of the time, Pallas kernels for 8%

profile of v4, /device:TPU:0, one launch (start us, length us, event | category | flops | bytes accessed | tf_op | source)
XLA Modules:
  0.0 78.7 jit_solution(4893890023638211600)
XLA Ops:
  0.0 0.0 copy-start.1
  0.0 0.0 copy-start
  0.0 0.0 copy-start.2
  0.0 2.6 %pack_heads.1 = bf16[8,4,64,128]{3,2,1,0:T(8,128)(2,1)} custom-call(bf16[8,64,4096]{2,1,0:T(8,128)(2,1)} %corpus_ref.1), custom_call_target="tpu_custom_call" | custom-call | tf_op jit(solution)/shard_map/pack_heads/pallas_call | solution.py:70
  2.7 5.9 %all-to-all-start.1 = ((bf16[8,4,64,128]{3,2,1,0:T(8,128)(2,1)}), bf16[8,4,64,128]{3,2,1,0:T(8,128)(2,1)S(1)}, u32[]{:S(2)}, u32[]{:S(2)}) async-start(bf16[8,4,64,128]{3,2,1,0:T(8,128)(2,1)} %pack_heads.1), calls=%async_computation.1 | async-start | bytes 1048576 | tf_op jit(solution)/shard_map/all_to_all | solution.py:305
  8.6 0.0 copy-done.1
  8.6 0.0 copy-done
  8.6 0.1 copy.10
  8.7 0.1 reshape.35
  8.8 0.0 collective-permute-start
  8.8 0.0 copy-done.2
  8.9 1.1 %collective-permute-done = s32[16]{0:T(128)S(1)} collective-permute-done((s32[16]{0:T(128)S(1)}, s32[16]{0:T(128)S(1)}, u32[]{:S(2)}, u32[]{:S(2)}) %collective-permute-start) | collective-permute-done | bytes 96 | tf_op jit(solution)/shard_map/ppermute | solution.py:289
  9.9 0.1 fusion.25
  10.0 0.6 broadcast_in_dim.16.extra_ref
  10.6 6.4 %project_queries.1 = bf16[32,72,256]{2,1,0:T(8,128)(2,1)} custom-call(bf16[256,2048]{1,0:T(8,128)(2,1)} %hidden_ref.1, f32[1,2048]{1,0:T(1,128)} %bitcast.12, bf16[8,256]{1,0:T(8,128)(2,1)} %broadcast_in_dim.16.extra_ref, bf16[2048,2048]{1,0:T(8,128)(2,1)} %weight_ref.1), custom_call_target="tpu_custom_call" | custom-call | tf_op jit(solution)/shard_map/project_queries/pallas_call | solution.py:138
  17.0 1.7 %all-to-all-done.1 = bf16[8,4,64,128]{3,2,1,0:T(8,128)(2,1)S(1)} async-done(((bf16[8,4,64,128]{3,2,1,0:T(8,128)(2,1)}), bf16[8,4,64,128]{3,2,1,0:T(8,128)(2,1)S(1)}, u32[]{:S(2)}, u32[]{:S(2)}) %all-to-all-start.1) | async-done | bytes 524320 | tf_op jit(solution)/shard_map/all_to_all | solution.py:305
  18.7 6.9 %all-to-all-start = ((bf16[32,72,256]{2,1,0:T(8,128)(2,1)}), bf16[32,72,256]{2,1,0:T(8,128)(2,1)S(1)}, u32[]{:S(2)}, u32[]{:S(2)}) async-start(bf16[32,72,256]{2,1,0:T(8,128)(2,1)} %project_queries.1), calls=%async_computation | async-start | bytes 2359296 | tf_op jit(solution)/shard_map/all_to_all | solution.py:310
  25.6 4.0 %collective-permute-start.2 = (bf16[32,64,128]{2,1,0:T(8,128)(2,1)S(1)}, bf16[32,64,128]{2,1,0:T(8,128)(2,1)S(1)}, u32[]{:S(2)}, u32[]{:S(2)}) collective-permute-start(bf16[32,64,128]{2,1,0:T(8,128)(2,1)S(1)} %bitcast.8), channel_id=1, source_target_pairs={{0,96},{96,0},{32,64},{64,32},{1,97},{97,1},{33,65},{65,33},{2,98}... | collective-permute-start | bytes 1572872 | tf_op jit(solution)/shard_map/ppermute | solution.py:306
  29.6 0.0 collective-permute-start.1
  29.6 11.7 %collective-permute-done.2.refs_2_ = bf16[32,64,128]{2,1,0:T(8,128)(2,1)S(1)} collective-permute-done((bf16[32,64,128]{2,1,0:T(8,128)(2,1)S(1)}, bf16[32,64,128]{2,1,0:T(8,128)(2,1)S(1)}, u32[]{:S(2)}, u32[]{:S(2)}) %collective-permute-start.2) | collective-permute-done | bytes 524320 | tf_op jit(solution)/shard_map/ppermute | solution.py:306
  41.3 0.0 collective-permute-start.3
  41.3 2.9 %all-to-all-done.q_ref = bf16[32,72,256]{2,1,0:T(8,128)(2,1)S(1)} async-done(((bf16[32,72,256]{2,1,0:T(8,128)(2,1)}), bf16[32,72,256]{2,1,0:T(8,128)(2,1)S(1)}, u32[]{:S(2)}, u32[]{:S(2)}) %all-to-all-start) | async-done | bytes 1179680 | tf_op jit(solution)/shard_map/all_to_all | solution.py:310
  44.3 0.1 fusion.7.ids_ref
  44.3 0.0 collective-permute-done.1.refs_1_
  44.3 0.0 collective-permute-done.3.refs_3_
  44.3 9.1 %attend.1 = (bf16[32,64,256]{2,1,0:T(8,128)(2,1)S(1)}, bf16[2048,2048]{1,0:T(8,128)(2,1)S(1)}) custom-call(s32[32,40]{1,0:T(8,128)S(1)} %fusion.7.ids_ref, bf16[32,72,256]{2,1,0:T(8,128)(2,1)S(1)} %all-to-all-done.q_ref, bf16[32,64,128]{2,1,0:T(8,128)(2,1)S(1)} %bitcast.10, bf16[32,64,128]{2,1,0:T(8,128)(2,1)S(1)} %collective-permute-done.1.refs_1_, ...), custom_call_target="tpu_custom_call" | custom-call | tf_op jit(solution)/shard_map/attend/pallas_call | solution.py:268
  53.5 21.9 %all_to_all.15 = bf16[32,64,256]{2,1,0:T(8,128)(2,1)S(1)} all-to-all(bf16[32,64,256]{2,1,0:T(8,128)(2,1)S(1)} %get-tuple-element.7), channel_id=1, replica_groups=mesh['zh'=2,'zl'=2,'y'=4,'x'=4,'c'=2] {'zl','y','x'}, dimensions={0} | all-to-all | bytes 2097152 | tf_op jit(solution)/shard_map/all_to_all | solution.py:319
  75.4 3.3 %project_output.1 = bf16[256,2048]{1,0:T(8,128)(2,1)} custom-call(bf16[2048,256]{1,0:T(8,128)(2,1)S(1)} %bitcast.7, bf16[2048,2048]{1,0:T(8,128)(2,1)S(1)} %get-tuple-element.8.weight_ref), custom_call_target="tpu_custom_call" | custom-call | tf_op jit(solution)/shard_map/project_output/pallas_call | solution.py:162
  (6 shorter events, 0.0 us)
Async XLA Ops:
  0.0 8.6 %copy-start.1 = (s32[1,1,8,2,1]{2,4,3,1,0:T(1,128)S(1)}, s32[1,1,8,2,1]{2,4,3,1,0:T(1,128)}, u32[]{:S(2)}) copy-start(s32[1,1,8,2,1]{2,4,3,1,0:T(1,128)} %param.13) | copy-start | bytes 196
  0.0 8.6 %copy-start = (s32[1,1,8,2]{2,3,1,0:T(2,128)S(1)}, s32[1,1,8,2]{2,3,1,0:T(2,128)}, u32[]{:S(2)}) copy-start(s32[1,1,8,2]{2,3,1,0:T(2,128)} %param.14) | copy-start | bytes 196
  0.0 8.8 %copy-start.2 = (s32[8]{0:T(128)S(1)}, s32[8]{0:T(128)}, u32[]{:S(2)}) copy-start(s32[8]{0:T(128)} %param.15) | copy-start | bytes 100
  2.7 16.0 %all-to-all-start.1 = ((bf16[8,4,64,128]{3,2,1,0:T(8,128)(2,1)}), bf16[8,4,64,128]{3,2,1,0:T(8,128)(2,1)S(1)}, u32[]{:S(2)}, u32[]{:S(2)}) async-start(bf16[8,4,64,128]{3,2,1,0:T(8,128)(2,1)} %pack_heads.1), calls=%async_computation.1 | async-start | bytes 1048576 | tf_op jit(solution)/shard_map/all_to_all | solution.py:305
  8.8 1.1 %collective-permute-start = (s32[16]{0:T(128)S(1)}, s32[16]{0:T(128)S(1)}, u32[]{:S(2)}, u32[]{:S(2)}) collective-permute-start(s32[16]{0:T(128)S(1)} %reshape.35), channel_id=1, source_target_pairs={{0,1},{1,0},{2,3},{3,2},{4,5},{5,4},{6,7},{7,6},{8,9},{9,8},{10,11... | collective-permute-start | bytes 200 | tf_op jit(solution)/shard_map/ppermute | solution.py:289
  18.7 25.6 %all-to-all-start = ((bf16[32,72,256]{2,1,0:T(8,128)(2,1)}), bf16[32,72,256]{2,1,0:T(8,128)(2,1)S(1)}, u32[]{:S(2)}, u32[]{:S(2)}) async-start(bf16[32,72,256]{2,1,0:T(8,128)(2,1)} %project_queries.1), calls=%async_computation | async-start | bytes 2359296 | tf_op jit(solution)/shard_map/all_to_all | solution.py:310
  25.6 15.7 %collective-permute-start.2 = (bf16[32,64,128]{2,1,0:T(8,128)(2,1)S(1)}, bf16[32,64,128]{2,1,0:T(8,128)(2,1)S(1)}, u32[]{:S(2)}, u32[]{:S(2)}) collective-permute-start(bf16[32,64,128]{2,1,0:T(8,128)(2,1)S(1)} %bitcast.8), channel_id=1, source_target_pairs={{0,96},{96,0},{32,64},{64,32},{1,97},{97,1},{33,65},{65,33},{2,98}... | collective-permute-start | bytes 1572872 | tf_op jit(solution)/shard_map/ppermute | solution.py:306
  29.6 14.7 %collective-permute-start.1 = (bf16[32,64,128]{2,1,0:T(8,128)(2,1)S(1)}, bf16[32,64,128]{2,1,0:T(8,128)(2,1)S(1)}, u32[]{:S(2)}, u32[]{:S(2)}) collective-permute-start(bf16[32,64,128]{2,1,0:T(8,128)(2,1)S(1)} %bitcast.9), channel_id=1, source_target_pairs={{0,1},{1,0},{2,3},{3,2},{4,5},{5,4},{6,7},{7,6},{8,9},{9,8},{10,11... | collective-permute-start | bytes 1572872 | tf_op jit(solution)/shard_map/ppermute | solution.py:289
  41.3 3.0 %collective-permute-start.3 = (bf16[32,64,128]{2,1,0:T(8,128)(2,1)S(1)}, bf16[32,64,128]{2,1,0:T(8,128)(2,1)S(1)}, u32[]{:S(2)}, u32[]{:S(2)}) collective-permute-start(bf16[32,64,128]{2,1,0:T(8,128)(2,1)S(1)} %collective-permute-done.2.refs_2_), channel_id=1, source_target_pairs={{0,1},{1,0},{2,3},{3,2},{4,5},{5,4},{6,7},{7,6},{8,9},{9,8},{10,11... | collective-permute-start | bytes 1572872 | tf_op jit(solution)/shard_map/ppermute | solution.py:289

commit v5 on v4

--- a/solution.py
+++ b/solution.py
@@ -10,6 +10,7 @@
 DH = 64
 P_SIZE = 64
 TQ = 256
+TILE = 512
 NEG = -1e30
 EXTRA = 8
 GROUP = 4
@@ -69,17 +70,17 @@
     block = (stored // 2, P_SIZE, 2 * DH)
     return pl.pallas_call(
         functools.partial(pack_kernel, n_x=n_x),
-        in_specs=[anywhere()],
+        in_specs=[pl.BlockSpec(memory_space=pltpu.HBM)],
         out_specs=whole(),
-        out_shape=jax.ShapeDtypeStruct((n_near,) + block, jnp.bfloat16),
+        out_shape=pltpu.VMEM((n_near,) + block, jnp.bfloat16),
         scratch_shapes=[
             pltpu.VMEM((n_near,) + block, jnp.bfloat16),
             pltpu.VMEM((n_near,) + block, jnp.bfloat16),
             pltpu.SemaphoreType.DMA((n_near, 2)),
         ],
-        compiler_params=pltpu.CompilerParams(vmem_limit_bytes=LIMIT),
+        compiler_params=pltpu.CompilerParams(vmem_limit_bytes=16 * 2**20),
         name="pack_heads",
-    )(corpus_kv)
+    )(pltpu.with_memory_space_constraint(corpus_kv, pltpu.HBM))
 
 
 def fetch(weight_ref, held_ref, sems, chunk_of):
@@ -137,24 +138,31 @@
     rows, width = hidden.shape
     return pl.pallas_call(
         query_kernel,
-        in_specs=[whole(), whole(), whole(), anywhere()],
+        in_specs=[whole(), whole(), whole(), pl.BlockSpec(memory_space=pltpu.HBM)],
         out_specs=whole(),
-        out_shape=jax.ShapeDtypeStruct((width // DH, DH + EXTRA, rows), jnp.bfloat16),
+        out_shape=pltpu.VMEM((width // DH, DH + EXTRA, rows), jnp.bfloat16),
         scratch_shapes=projection_scratch(rows, width),
-        compiler_params=pltpu.CompilerParams(vmem_limit_bytes=LIMIT),
+        compiler_params=pltpu.CompilerParams(vmem_limit_bytes=32 * 2**20),
         name="project_queries",
-    )(hidden, gain.reshape(1, width), extra, weight)
-
-
-def output_kernel(attended_ref, weight_ref, out_ref, rows_ref):
+    )(hidden, gain.reshape(1, width), extra, pltpu.with_memory_space_constraint(weight, pltpu.HBM))
+
+
+def output_kernel(attended_ref, weight_ref, out_ref, rows_ref, tile_ref, sems):
     width = weight_ref.shape[1]
+    copies = []
     for n in range(0, width, TQ):
         rows_ref[:, n : n + TQ] = attended_ref[n : n + TQ, :].T
-    for n in range(0, width, TQ):
-        columns = slice(n, n + TQ)
-        out_ref[:, columns] = jnp.dot(
+    for n in range(width // TILE):
+        columns = slice(n * TILE, (n + 1) * TILE)
+        tile_ref[n] = jnp.dot(
             rows_ref[...], weight_ref[:, columns], preferred_element_type=jnp.float32
         ).astype(jnp.bfloat16)
+        copies.append(
+            pltpu.make_async_copy(tile_ref.at[n], out_ref.at[:, pl.ds(n * TILE, TILE)], sems.at[n])
+        )
+        copies[-1].start()
+    for copy in copies:
+        copy.wait()
 
 
 def project_output(attended, weight):
@@ -162,9 +170,13 @@
     return pl.pallas_call(
         output_kernel,
         in_specs=[whole(), whole()],
-        out_specs=whole(),
+        out_specs=pl.BlockSpec(memory_space=pltpu.HBM),
         out_shape=jax.ShapeDtypeStruct((rows, width), jnp.bfloat16),
-        scratch_shapes=[pltpu.VMEM((rows, width), jnp.bfloat16)],
+        scratch_shapes=[
+            pltpu.VMEM((rows, width), jnp.bfloat16),
+            pltpu.VMEM((width // TILE, rows, TILE), jnp.bfloat16),
+            pltpu.SemaphoreType.DMA((width // TILE,)),
+        ],
         compiler_params=pltpu.CompilerParams(vmem_limit_bytes=16 * 2**20),
         name="project_output",
     )(attended, pltpu.with_memory_space_constraint(weight, pltpu.VMEM))

time: 79.6 us -> 78.3 us (0.984)
  Pallas kernels: 21.5 us -> 19.1 us
  blocking collectives: 21.9 us -> 23.4 us
  starting transfers between devices: 16.9 us -> 15.5 us
  waiting for transfers between devices: 17.4 us -> 18.7 us
    all_to_all x1, waiting for transfers between devices: 1.65 us -> 3.44 us  [body(): lax.all_to_all(packed, NEAR_AXES, 0, 0, tiled=True)]
    all_to_all x1, blocking collectives: 21.9 us -> 23.4 us  [body(): attended = lax.all_to_all(attended, HEAD_AXES, 0, 0, tiled=True)]
    pallas_call x3, Pallas kernels: 12.4 us -> 11 us  [the longest x1 5.18 us: project_queries(): pl.pallas_call(query_kernel, in_specs=[whole(), whole(), whole(), pl.Bloc...]
    all_to_all x1, starting transfers between devices: 6.92 us -> 5.59 us  [body(): queries = lax.all_to_all(queries, HEAD_AXES, 0, 0, tiled=True)]
    pallas_call x1, Pallas kernels: 9.14 us -> 8.11 us  [attend(): pl.pallas_call(functools.partial(attend_kernel, n_x=n_x), in_specs=[pl.Bl...]
  transfers between devices with their start and end apart: 6 -> 6, of which waited for: 4 -> 4; matrix products, arithmetic and copies ran while one was open for 1% -> 0% of each run, Pallas kernels for 8% -> 7%
where the time goes in v5:
time: 78.3 us; the launch traced here: 77.3 us
  blocking collectives  23.4 us (30%)
  Pallas kernels  19.1 us (24%)
  waiting for transfers between devices  18.7 us (24%)
  starting transfers between devices  15.5 us (20%)
    all_to_all x1, blocking collectives, body(): attended = lax.all_to_all(attended, HEAD_AXES, 0, 0, tiled=True)  23.4 us
    ppermute x1, waiting for transfers between devices, body(): far = lax.ppermute(near, ('zh', 'zl'), [(0, 3), (3, 0), (1, 2), (2, 1)])  11.3 us
    pallas_call x1, Pallas kernels, attend(): pl.pallas_call(functools.partial(attend_kernel, n_x=n_x), in_specs=[pl.Bl...  8.11 us
    all_to_all x1, starting transfers between devices, body(): lax.all_to_all(packed, NEAR_AXES, 0, 0, tiled=True)  5.9 us
    all_to_all x1, starting transfers between devices, body(): queries = lax.all_to_all(queries, HEAD_AXES, 0, 0, tiled=True)  5.59 us
    pallas_call x1, Pallas kernels, project_queries(): pl.pallas_call(query_kernel, in_specs=[whole(), whole(), whole(), pl.Bloc...  5.18 us
    ppermute x1, starting transfers between devices, body(): far = lax.ppermute(near, ('zh', 'zl'), [(0, 3), (3, 0), (1, 2), (2, 1)])  4 us
    all_to_all x1, waiting for transfers between devices, body(): lax.all_to_all(packed, NEAR_AXES, 0, 0, tiled=True)  3.44 us
  transfers between devices with their start and end apart: 6, of which 4 were waited for; matrix products, arithmetic and copies ran while one was open for 0% of the time, Pallas kernels for 7%

profile of v5, /device:TPU:0, one launch (start us, length us, event | category | flops | bytes accessed | tf_op | source)
XLA Modules:
  0.0 77.3 jit_solution(9597367227409746561)
XLA Ops:
  0.0 0.0 copy-start.3
  0.0 0.0 copy-start.2
  0.0 0.0 copy-start.4
  0.0 0.0 copy-start.1
  0.0 0.0 copy-start
  0.0 2.7 %pack_heads.1 = bf16[8,4,64,128]{3,2,1,0:T(8,128)(2,1)} custom-call(bf16[8,64,4096]{2,1,0:T(8,128)(2,1)} %corpus_ref.1), custom_call_target="tpu_custom_call" | custom-call | tf_op jit(solution)/shard_map/pack_heads/pallas_call | solution.py:71
  2.8 5.9 %all-to-all-start.1 = ((bf16[8,4,64,128]{3,2,1,0:T(8,128)(2,1)}), bf16[8,4,64,128]{3,2,1,0:T(8,128)(2,1)S(1)}, u32[]{:S(2)}, u32[]{:S(2)}) async-start(bf16[8,4,64,128]{3,2,1,0:T(8,128)(2,1)} %pack_heads.1), calls=%async_computation.1 | async-start | bytes 1048576 | tf_op jit(solution)/shard_map/all_to_all | solution.py:317
  8.7 0.0 copy-done.3
  8.7 0.0 copy-done.2
  8.7 0.1 copy.10
  8.8 0.1 reshape.35
  8.9 0.0 collective-permute-start
  8.9 0.0 copy-done.4
  8.9 1.1 %collective-permute-done = s32[16]{0:T(128)S(1)} collective-permute-done((s32[16]{0:T(128)S(1)}, s32[16]{0:T(128)S(1)}, u32[]{:S(2)}, u32[]{:S(2)}) %collective-permute-start) | collective-permute-done | bytes 96 | tf_op jit(solution)/shard_map/ppermute | solution.py:301
  10.0 0.1 fusion.25
  10.1 0.0 copy-done.1
  10.1 0.0 copy-done
  10.1 5.2 %project_queries.1 = bf16[32,72,256]{2,1,0:T(8,128)(2,1)} custom-call(bf16[256,2048]{1,0:T(8,128)(2,1)S(1)} %copy-done, f32[1,2048]{1,0:T(1,128)S(1)} %bitcast.11, bf16[8,256]{1,0:T(8,128)(2,1)S(1)} %broadcast_in_dim.16.extra_ref, bf16[2048,2048]{1,0:T(8,128)(2,1)} %weight_ref.1), custom_call_target="tpu_custom_call" | custom-call | tf_op jit(solution)/shard_map/project_queries/pallas_call | solution.py:139
  15.3 3.4 %all-to-all-done.1 = bf16[8,4,64,128]{3,2,1,0:T(8,128)(2,1)S(1)} async-done(((bf16[8,4,64,128]{3,2,1,0:T(8,128)(2,1)}), bf16[8,4,64,128]{3,2,1,0:T(8,128)(2,1)S(1)}, u32[]{:S(2)}, u32[]{:S(2)}) %all-to-all-start.1) | async-done | bytes 524320 | tf_op jit(solution)/shard_map/all_to_all | solution.py:317
  18.8 5.6 %all-to-all-start = ((bf16[32,72,256]{2,1,0:T(8,128)(2,1)}), bf16[32,72,256]{2,1,0:T(8,128)(2,1)S(1)}, u32[]{:S(2)}, u32[]{:S(2)}) async-start(bf16[32,72,256]{2,1,0:T(8,128)(2,1)} %project_queries.1), calls=%async_computation | async-start | bytes 2359296 | tf_op jit(solution)/shard_map/all_to_all | solution.py:322
  24.3 4.0 %collective-permute-start.2 = (bf16[32,64,128]{2,1,0:T(8,128)(2,1)S(1)}, bf16[32,64,128]{2,1,0:T(8,128)(2,1)S(1)}, u32[]{:S(2)}, u32[]{:S(2)}) collective-permute-start(bf16[32,64,128]{2,1,0:T(8,128)(2,1)S(1)} %bitcast.8), channel_id=1, source_target_pairs={{0,96},{96,0},{32,64},{64,32},{1,97},{97,1},{33,65},{65,33},{2,98}... | collective-permute-start | bytes 1572872 | tf_op jit(solution)/shard_map/ppermute | solution.py:318
  28.3 0.0 collective-permute-start.1
  28.3 11.3 %collective-permute-done.2.refs_2_ = bf16[32,64,128]{2,1,0:T(8,128)(2,1)S(1)} collective-permute-done((bf16[32,64,128]{2,1,0:T(8,128)(2,1)S(1)}, bf16[32,64,128]{2,1,0:T(8,128)(2,1)S(1)}, u32[]{:S(2)}, u32[]{:S(2)}) %collective-permute-start.2) | collective-permute-done | bytes 524320 | tf_op jit(solution)/shard_map/ppermute | solution.py:318
  39.6 0.0 collective-permute-start.3
  39.6 2.9 %all-to-all-done.q_ref = bf16[32,72,256]{2,1,0:T(8,128)(2,1)S(1)} async-done(((bf16[32,72,256]{2,1,0:T(8,128)(2,1)}), bf16[32,72,256]{2,1,0:T(8,128)(2,1)S(1)}, u32[]{:S(2)}, u32[]{:S(2)}) %all-to-all-start) | async-done | bytes 1179680 | tf_op jit(solution)/shard_map/all_to_all | solution.py:322
  42.5 0.1 fusion.7.ids_ref
  42.6 0.0 collective-permute-done.1.refs_1_
  42.6 0.0 collective-permute-done.3.refs_3_
  42.6 8.1 %attend.1 = (bf16[32,64,256]{2,1,0:T(8,128)(2,1)S(1)}, bf16[2048,2048]{1,0:T(8,128)(2,1)S(1)}) custom-call(s32[32,40]{1,0:T(8,128)S(1)} %fusion.7.ids_ref, bf16[32,72,256]{2,1,0:T(8,128)(2,1)S(1)} %all-to-all-done.q_ref, bf16[32,64,128]{2,1,0:T(8,128)(2,1)S(1)} %bitcast.10, bf16[32,64,128]{2,1,0:T(8,128)(2,1)S(1)} %collective-permute-done.1.refs_1_, ...), custom_call_target="tpu_custom_call" | custom-call | tf_op jit(solution)/shard_map/attend/pallas_call | solution.py:280
  50.7 23.4 %all_to_all.15 = bf16[32,64,256]{2,1,0:T(8,128)(2,1)S(1)} all-to-all(bf16[32,64,256]{2,1,0:T(8,128)(2,1)S(1)} %get-tuple-element.7), channel_id=1, replica_groups=mesh['zh'=2,'zl'=2,'y'=4,'x'=4,'c'=2] {'zl','y','x'}, dimensions={0} | all-to-all | bytes 2097152 | tf_op jit(solution)/shard_map/all_to_all | solution.py:331
  74.2 3.1 %project_output.1 = bf16[256,2048]{1,0:T(8,128)(2,1)} custom-call(bf16[2048,256]{1,0:T(8,128)(2,1)S(1)} %bitcast.7, bf16[2048,2048]{1,0:T(8,128)(2,1)S(1)} %get-tuple-element.8.weight_ref), custom_call_target="tpu_custom_call" | custom-call | tf_op jit(solution)/shard_map/project_output/pallas_call | solution.py:170
  (7 shorter events, 0.0 us)
Async XLA Ops:
  0.0 8.7 %copy-start.3 = (s32[1,1,8,2,1]{2,4,3,1,0:T(1,128)S(1)}, s32[1,1,8,2,1]{2,4,3,1,0:T(1,128)}, u32[]{:S(2)}) copy-start(s32[1,1,8,2,1]{2,4,3,1,0:T(1,128)} %param.13) | copy-start | bytes 196
  0.0 8.7 %copy-start.2 = (s32[1,1,8,2]{2,3,1,0:T(2,128)S(1)}, s32[1,1,8,2]{2,3,1,0:T(2,128)}, u32[]{:S(2)}) copy-start(s32[1,1,8,2]{2,3,1,0:T(2,128)} %param.14) | copy-start | bytes 196
  0.0 8.9 %copy-start.4 = (s32[8]{0:T(128)S(1)}, s32[8]{0:T(128)}, u32[]{:S(2)}) copy-start(s32[8]{0:T(128)} %param.15) | copy-start | bytes 100
  0.0 10.1 %copy-start.1 = (f32[2048]{0:T(1024)S(1)}, f32[2048]{0:T(1024)}, u32[]{:S(2)}) copy-start(f32[2048]{0:T(1024)} %param.9) | copy-start | bytes 24580
  0.0 10.1 %copy-start = (bf16[256,2048]{1,0:T(8,128)(2,1)S(1)}, bf16[256,2048]{1,0:T(8,128)(2,1)}, u32[]{:S(2)}) copy-start(bf16[256,2048]{1,0:T(8,128)(2,1)} %hidden_ref.1) | copy-start | bytes 3145732
  2.8 16.0 %all-to-all-start.1 = ((bf16[8,4,64,128]{3,2,1,0:T(8,128)(2,1)}), bf16[8,4,64,128]{3,2,1,0:T(8,128)(2,1)S(1)}, u32[]{:S(2)}, u32[]{:S(2)}) async-start(bf16[8,4,64,128]{3,2,1,0:T(8,128)(2,1)} %pack_heads.1), calls=%async_computation.1 | async-start | bytes 1048576 | tf_op jit(solution)/shard_map/all_to_all | solution.py:317
  8.9 1.1 %collective-permute-start = (s32[16]{0:T(128)S(1)}, s32[16]{0:T(128)S(1)}, u32[]{:S(2)}, u32[]{:S(2)}) collective-permute-start(s32[16]{0:T(128)S(1)} %reshape.35), channel_id=1, source_target_pairs={{0,1},{1,0},{2,3},{3,2},{4,5},{5,4},{6,7},{7,6},{8,9},{9,8},{10,11... | collective-permute-start | bytes 200 | tf_op jit(solution)/shard_map/ppermute | solution.py:301
  18.8 23.8 %all-to-all-start = ((bf16[32,72,256]{2,1,0:T(8,128)(2,1)}), bf16[32,72,256]{2,1,0:T(8,128)(2,1)S(1)}, u32[]{:S(2)}, u32[]{:S(2)}) async-start(bf16[32,72,256]{2,1,0:T(8,128)(2,1)} %project_queries.1), calls=%async_computation | async-start | bytes 2359296 | tf_op jit(solution)/shard_map/all_to_all | solution.py:322
  24.3 15.3 %collective-permute-start.2 = (bf16[32,64,128]{2,1,0:T(8,128)(2,1)S(1)}, bf16[32,64,128]{2,1,0:T(8,128)(2,1)S(1)}, u32[]{:S(2)}, u32[]{:S(2)}) collective-permute-start(bf16[32,64,128]{2,1,0:T(8,128)(2,1)S(1)} %bitcast.8), channel_id=1, source_target_pairs={{0,96},{96,0},{32,64},{64,32},{1,97},{97,1},{33,65},{65,33},{2,98}... | collective-permute-start | bytes 1572872 | tf_op jit(solution)/shard_map/ppermute | solution.py:318
  28.3 14.3 %collective-permute-start.1 = (bf16[32,64,128]{2,1,0:T(8,128)(2,1)S(1)}, bf16[32,64,128]{2,1,0:T(8,128)(2,1)S(1)}, u32[]{:S(2)}, u32[]{:S(2)}) collective-permute-start(bf16[32,64,128]{2,1,0:T(8,128)(2,1)S(1)} %bitcast.9), channel_id=1, source_target_pairs={{0,1},{1,0},{2,3},{3,2},{4,5},{5,4},{6,7},{7,6},{8,9},{9,8},{10,11... | collective-permute-start | bytes 1572872 | tf_op jit(solution)/shard_map/ppermute | solution.py:301
  39.6 3.0 %collective-permute-start.3 = (bf16[32,64,128]{2,1,0:T(8,128)(2,1)S(1)}, bf16[32,64,128]{2,1,0:T(8,128)(2,1)S(1)}, u32[]{:S(2)}, u32[]{:S(2)}) collective-permute-start(bf16[32,64,128]{2,1,0:T(8,128)(2,1)S(1)} %collective-permute-done.2.refs_2_), channel_id=1, source_target_pairs={{0,1},{1,0},{2,3},{3,2},{4,5},{5,4},{6,7},{7,6},{8,9},{9,8},{10,11... | collective-permute-start | bytes 1572872 | tf_op jit(solution)/shard_map/ppermute | solution.py:301

commit v6 on v5

--- a/solution.py
+++ b/solution.py
@@ -16,7 +16,7 @@
 GROUP = 4
 SIDE = 8
 HEAD_AXES = ("zl", "y", "x")
-NEAR_AXES = ("zl", "y")
+NEAR_AXES = ("y", "zl")
 OWNER_AXES = ("zh", "zl", "y")
 EVERY = ("zh", "zl", "y", "x", "c")
 LIMIT = 60 * 2**20
@@ -40,7 +40,8 @@
     width = corpus_ref.shape[2] // 2
     copies = []
     for i in range(n_near):
-        column = pl.multiple_of((turned(i, n_near, far) * n_x + x) // 2 * 128, 128)
+        head = turned(i % 2 * (n_near // 2) + i // 2, n_near, far)
+        column = pl.multiple_of((head * n_x + x) // 2 * 128, 128)
         for n, (held, offset) in enumerate(((key_ref, 0), (value_ref, width))):
             copies.append(
                 pltpu.make_async_copy(
@@ -324,7 +325,8 @@
     half = stored // 2
     owner, local = ids // stored, ids % stored
     part = (owner // n_near ^ far_index) * 2 + (local // half ^ core)
-    place = (part * n_near + owner % n_near) * half + local % half
+    near_place = owner % (n_near // 2) * 2 + owner % n_near // (n_near // 2)
+    place = (part * n_near + near_place) * half + local % half
     ids = jnp.where(jnp.arange(entries)[None, :] < 2 * wanted.shape[0], place, ids)
 
     attended, weight = attend(ids, queries, parts, out_weight, n_x)

time: 78.3 us -> 78.6 us (level)
  no operation moved by 1% of the time
where the time goes in v6:
time: 78.6 us; the launch traced here: 78.4 us
  blocking collectives  24 us (31%)
  Pallas kernels  19.6 us (25%)
  waiting for transfers between devices  18.1 us (23%)
  starting transfers between devices  16.1 us (20%)
    all_to_all x1, blocking collectives, body(): attended = lax.all_to_all(attended, HEAD_AXES, 0, 0, tiled=True)  24 us
    ppermute x1, waiting for transfers between devices, body(): far = lax.ppermute(near, ('zh', 'zl'), [(0, 3), (3, 0), (1, 2), (2, 1)])  11.3 us
    pallas_call x1, Pallas kernels, attend(): pl.pallas_call(functools.partial(attend_kernel, n_x=n_x), in_specs=[pl.Bl...  8.61 us
    all_to_all x1, starting transfers between devices, body(): queries = lax.all_to_all(queries, HEAD_AXES, 0, 0, tiled=True)  6.19 us
    all_to_all x1, starting transfers between devices, body(): lax.all_to_all(packed, NEAR_AXES, 0, 0, tiled=True)  5.9 us
    pallas_call x1, Pallas kernels, project_queries(): pl.pallas_call(query_kernel, in_specs=[whole(), whole(), whole(), pl.Bloc...  5.18 us
    ppermute x1, starting transfers between devices, body(): far = lax.ppermute(near, ('zh', 'zl'), [(0, 3), (3, 0), (1, 2), (2, 1)])  4 us
    pallas_call x1, Pallas kernels, project_output(): pl.pallas_call(output_kernel, in_specs=[whole(), whole()], out_specs=pl.B...  3.09 us
  transfers between devices with their start and end apart: 6, of which 4 were waited for; matrix products, arithmetic and copies ran while one was open for 0% of the time, Pallas kernels for 7%

profile of v6, /device:TPU:0, one launch (start us, length us, event | category | flops | bytes accessed | tf_op | source)
XLA Modules:
  0.0 78.4 jit_solution(10061758009630428434)
XLA Ops:
  0.0 0.0 copy-start.3
  0.0 0.0 copy-start.2
  0.0 0.0 copy-start.4
  0.0 0.0 copy-start.1
  0.0 0.0 copy-start
  0.0 2.7 %pack_heads.1 = bf16[8,4,64,128]{3,2,1,0:T(8,128)(2,1)} custom-call(bf16[8,64,4096]{2,1,0:T(8,128)(2,1)} %corpus_ref.1), custom_call_target="tpu_custom_call" | custom-call | tf_op jit(solution)/shard_map/pack_heads/pallas_call | solution.py:72
  2.8 5.9 %all-to-all-start.1 = ((bf16[8,4,64,128]{3,2,1,0:T(8,128)(2,1)}), bf16[8,4,64,128]{3,2,1,0:T(8,128)(2,1)S(1)}, u32[]{:S(2)}, u32[]{:S(2)}) async-start(bf16[8,4,64,128]{3,2,1,0:T(8,128)(2,1)} %pack_heads.1), calls=%async_computation.1 | async-start | bytes 1048576 | tf_op jit(solution)/shard_map/all_to_all | solution.py:318
  8.7 0.0 copy-done.3
  8.7 0.0 copy-done.2
  8.7 0.1 copy.10
  8.8 0.1 reshape.35
  8.9 0.0 collective-permute-start
  8.9 0.0 copy-done.4
  8.9 1.1 %collective-permute-done = s32[16]{0:T(128)S(1)} collective-permute-done((s32[16]{0:T(128)S(1)}, s32[16]{0:T(128)S(1)}, u32[]{:S(2)}, u32[]{:S(2)}) %collective-permute-start) | collective-permute-done | bytes 96 | tf_op jit(solution)/shard_map/ppermute | solution.py:302
  10.0 0.1 fusion.28
  10.1 0.0 copy-done.1
  10.1 0.0 copy-done
  10.1 5.2 %project_queries.1 = bf16[32,72,256]{2,1,0:T(8,128)(2,1)} custom-call(bf16[256,2048]{1,0:T(8,128)(2,1)S(1)} %copy-done, f32[1,2048]{1,0:T(1,128)S(1)} %bitcast.11, bf16[8,256]{1,0:T(8,128)(2,1)S(1)} %broadcast_in_dim.16.extra_ref, bf16[2048,2048]{1,0:T(8,128)(2,1)} %weight_ref.1), custom_call_target="tpu_custom_call" | custom-call | tf_op jit(solution)/shard_map/project_queries/pallas_call | solution.py:140
  15.3 2.8 %all-to-all-done.1 = bf16[8,4,64,128]{3,2,1,0:T(8,128)(2,1)S(1)} async-done(((bf16[8,4,64,128]{3,2,1,0:T(8,128)(2,1)}), bf16[8,4,64,128]{3,2,1,0:T(8,128)(2,1)S(1)}, u32[]{:S(2)}, u32[]{:S(2)}) %all-to-all-start.1) | async-done | bytes 524320 | tf_op jit(solution)/shard_map/all_to_all | solution.py:318
  18.1 6.2 %all-to-all-start = ((bf16[32,72,256]{2,1,0:T(8,128)(2,1)}), bf16[32,72,256]{2,1,0:T(8,128)(2,1)S(1)}, u32[]{:S(2)}, u32[]{:S(2)}) async-start(bf16[32,72,256]{2,1,0:T(8,128)(2,1)} %project_queries.1), calls=%async_computation | async-start | bytes 2359296 | tf_op jit(solution)/shard_map/all_to_all | solution.py:323
  24.3 4.0 %collective-permute-start.2 = (bf16[32,64,128]{2,1,0:T(8,128)(2,1)S(1)}, bf16[32,64,128]{2,1,0:T(8,128)(2,1)S(1)}, u32[]{:S(2)}, u32[]{:S(2)}) collective-permute-start(bf16[32,64,128]{2,1,0:T(8,128)(2,1)S(1)} %bitcast.8), channel_id=1, source_target_pairs={{0,96},{96,0},{32,64},{64,32},{1,97},{97,1},{33,65},{65,33},{2,98}... | collective-permute-start | bytes 1572872 | tf_op jit(solution)/shard_map/ppermute | solution.py:319
  28.3 0.0 collective-permute-start.1
  28.3 11.3 %collective-permute-done.2.refs_2_ = bf16[32,64,128]{2,1,0:T(8,128)(2,1)S(1)} collective-permute-done((bf16[32,64,128]{2,1,0:T(8,128)(2,1)S(1)}, bf16[32,64,128]{2,1,0:T(8,128)(2,1)S(1)}, u32[]{:S(2)}, u32[]{:S(2)}) %collective-permute-start.2) | collective-permute-done | bytes 524320 | tf_op jit(solution)/shard_map/ppermute | solution.py:319
  39.6 0.0 collective-permute-start.3
  39.6 2.9 %all-to-all-done.q_ref = bf16[32,72,256]{2,1,0:T(8,128)(2,1)S(1)} async-done(((bf16[32,72,256]{2,1,0:T(8,128)(2,1)}), bf16[32,72,256]{2,1,0:T(8,128)(2,1)S(1)}, u32[]{:S(2)}, u32[]{:S(2)}) %all-to-all-start) | async-done | bytes 1179680 | tf_op jit(solution)/shard_map/all_to_all | solution.py:323
  42.5 0.1 fusion.7.ids_ref
  42.6 0.0 collective-permute-done.1.refs_1_
  42.6 0.0 collective-permute-done.3.refs_3_
  42.6 8.6 %attend.1 = (bf16[32,64,256]{2,1,0:T(8,128)(2,1)S(1)}, bf16[2048,2048]{1,0:T(8,128)(2,1)S(1)}) custom-call(s32[32,40]{1,0:T(8,128)S(1)} %fusion.7.ids_ref, bf16[32,72,256]{2,1,0:T(8,128)(2,1)S(1)} %all-to-all-done.q_ref, bf16[32,64,128]{2,1,0:T(8,128)(2,1)S(1)} %bitcast.10, bf16[32,64,128]{2,1,0:T(8,128)(2,1)S(1)} %collective-permute-done.1.refs_1_, ...), custom_call_target="tpu_custom_call" | custom-call | tf_op jit(solution)/shard_map/attend/pallas_call | solution.py:281
  51.3 24.0 %all_to_all.15 = bf16[32,64,256]{2,1,0:T(8,128)(2,1)S(1)} all-to-all(bf16[32,64,256]{2,1,0:T(8,128)(2,1)S(1)} %get-tuple-element.7), channel_id=1, replica_groups=mesh['zh'=2,'zl'=2,'y'=4,'x'=4,'c'=2] {'zl','y','x'}, dimensions={0} | all-to-all | bytes 2097152 | tf_op jit(solution)/shard_map/all_to_all | solution.py:333
  75.3 3.1 %project_output.1 = bf16[256,2048]{1,0:T(8,128)(2,1)} custom-call(bf16[2048,256]{1,0:T(8,128)(2,1)S(1)} %bitcast.7, bf16[2048,2048]{1,0:T(8,128)(2,1)S(1)} %get-tuple-element.8.weight_ref), custom_call_target="tpu_custom_call" | custom-call | tf_op jit(solution)/shard_map/project_output/pallas_call | solution.py:171
  (7 shorter events, 0.0 us)
Async XLA Ops:
  0.0 8.7 %copy-start.3 = (s32[1,1,8,2,1]{2,4,3,1,0:T(1,128)S(1)}, s32[1,1,8,2,1]{2,4,3,1,0:T(1,128)}, u32[]{:S(2)}) copy-start(s32[1,1,8,2,1]{2,4,3,1,0:T(1,128)} %param.13) | copy-start | bytes 196
  0.0 8.7 %copy-start.2 = (s32[1,1,8,2]{2,3,1,0:T(2,128)S(1)}, s32[1,1,8,2]{2,3,1,0:T(2,128)}, u32[]{:S(2)}) copy-start(s32[1,1,8,2]{2,3,1,0:T(2,128)} %param.14) | copy-start | bytes 196
  0.0 8.9 %copy-start.4 = (s32[8]{0:T(128)S(1)}, s32[8]{0:T(128)}, u32[]{:S(2)}) copy-start(s32[8]{0:T(128)} %param.15) | copy-start | bytes 100
  0.0 10.1 %copy-start.1 = (f32[2048]{0:T(1024)S(1)}, f32[2048]{0:T(1024)}, u32[]{:S(2)}) copy-start(f32[2048]{0:T(1024)} %param.9) | copy-start | bytes 24580
  0.0 10.1 %copy-start = (bf16[256,2048]{1,0:T(8,128)(2,1)S(1)}, bf16[256,2048]{1,0:T(8,128)(2,1)}, u32[]{:S(2)}) copy-start(bf16[256,2048]{1,0:T(8,128)(2,1)} %hidden_ref.1) | copy-start | bytes 3145732
  2.8 15.4 %all-to-all-start.1 = ((bf16[8,4,64,128]{3,2,1,0:T(8,128)(2,1)}), bf16[8,4,64,128]{3,2,1,0:T(8,128)(2,1)S(1)}, u32[]{:S(2)}, u32[]{:S(2)}) async-start(bf16[8,4,64,128]{3,2,1,0:T(8,128)(2,1)} %pack_heads.1), calls=%async_computation.1 | async-start | bytes 1048576 | tf_op jit(solution)/shard_map/all_to_all | solution.py:318
  8.9 1.1 %collective-permute-start = (s32[16]{0:T(128)S(1)}, s32[16]{0:T(128)S(1)}, u32[]{:S(2)}, u32[]{:S(2)}) collective-permute-start(s32[16]{0:T(128)S(1)} %reshape.35), channel_id=1, source_target_pairs={{0,1},{1,0},{2,3},{3,2},{4,5},{5,4},{6,7},{7,6},{8,9},{9,8},{10,11... | collective-permute-start | bytes 200 | tf_op jit(solution)/shard_map/ppermute | solution.py:302
  18.1 24.4 %all-to-all-start = ((bf16[32,72,256]{2,1,0:T(8,128)(2,1)}), bf16[32,72,256]{2,1,0:T(8,128)(2,1)S(1)}, u32[]{:S(2)}, u32[]{:S(2)}) async-start(bf16[32,72,256]{2,1,0:T(8,128)(2,1)} %project_queries.1), calls=%async_computation | async-start | bytes 2359296 | tf_op jit(solution)/shard_map/all_to_all | solution.py:323
  24.3 15.3 %collective-permute-start.2 = (bf16[32,64,128]{2,1,0:T(8,128)(2,1)S(1)}, bf16[32,64,128]{2,1,0:T(8,128)(2,1)S(1)}, u32[]{:S(2)}, u32[]{:S(2)}) collective-permute-start(bf16[32,64,128]{2,1,0:T(8,128)(2,1)S(1)} %bitcast.8), channel_id=1, source_target_pairs={{0,96},{96,0},{32,64},{64,32},{1,97},{97,1},{33,65},{65,33},{2,98}... | collective-permute-start | bytes 1572872 | tf_op jit(solution)/shard_map/ppermute | solution.py:319
  28.3 14.3 %collective-permute-start.1 = (bf16[32,64,128]{2,1,0:T(8,128)(2,1)S(1)}, bf16[32,64,128]{2,1,0:T(8,128)(2,1)S(1)}, u32[]{:S(2)}, u32[]{:S(2)}) collective-permute-start(bf16[32,64,128]{2,1,0:T(8,128)(2,1)S(1)} %bitcast.9), channel_id=1, source_target_pairs={{0,1},{1,0},{2,3},{3,2},{4,5},{5,4},{6,7},{7,6},{8,9},{9,8},{10,11... | collective-permute-start | bytes 1572872 | tf_op jit(solution)/shard_map/ppermute | solution.py:302
  39.6 3.0 %collective-permute-start.3 = (bf16[32,64,128]{2,1,0:T(8,128)(2,1)S(1)}, bf16[32,64,128]{2,1,0:T(8,128)(2,1)S(1)}, u32[]{:S(2)}, u32[]{:S(2)}) collective-permute-start(bf16[32,64,128]{2,1,0:T(8,128)(2,1)S(1)} %collective-permute-done.2.refs_2_), channel_id=1, source_target_pairs={{0,1},{1,0},{2,3},{3,2},{4,5},{5,4},{6,7},{7,6},{8,9},{9,8},{10,11... | collective-permute-start | bytes 1572872 | tf_op jit(solution)/shard_map/ppermute | solution.py:302
